TPU v7x, 32 devices: a whole 2x2x4 slice. The times are simulated.
32 devices in a mesh: ctx: 8 (over y, x, core), wsh: 4 (over z).
Axes of the slice: x: 2, y: 2, z: 4, core: 2. Of those that a mesh axis runs over, the one named last changes fastest.
Arguments:
- tokens: bfloat16 [8, 1024, 768], P('wsh', 'ctx'), may hold values from -6 to 6
- key_mask: int32 [8, 1024], P('wsh', 'ctx'), may hold values from 0 to 1, as said below
- w_qkv: bfloat16 [768, 2304], P('wsh'), may hold values from -0.3125 to 0.3125
- w_attn_out: bfloat16 [768, 768], P('wsh'), may hold values from -0.5 to 0.5
- w_in: bfloat16 [768, 2304], P('wsh'), may hold values from -0.21875 to 0.21875
- w_out: bfloat16 [1152, 768], P('wsh'), may hold values from -0.1875 to 0.1875
- attn_gain: bfloat16 [768], P('wsh'), may hold values from 0.099609375 to 1.8984375
- mlp_gain: bfloat16 [768], P('wsh'), may hold values from 0.099609375 to 1.8984375
- cotangent: bfloat16 [8, 1024, 768], P('wsh', 'ctx'), may hold values from -6 to 6
Outputs:
- output: bfloat16 [8, 1024, 768], P('wsh', 'ctx')
- grad_tokens: bfloat16 [8, 1024, 768], P('wsh', 'ctx')
- attn_gain_grad: float32 [768], P('wsh')
- mlp_gain_grad: float32 [768], P('wsh')
- w_qkv_grad: float32 [768, 2304], P('wsh')
- w_attn_out_grad: float32 [768, 768], P('wsh')
- w_in_grad: float32 [768, 2304], P('wsh')
- w_out_grad: float32 [1152, 768], P('wsh')
Inputs may be any that keep to these rules, and one draw needn't show every extreme that they name: `key_mask`: in each sequence the ones form a prefix that ends within the last 128 positions, and the last position is 0.
All inputs are finite; a program needn't handle non-finite values.
Results may differ from a plain program's by a relative error of at most 0.02.
Values may be sent and summed in bfloat16 or wider, within the bound.
A program may use at most 256 MiB of HBM per device.

v0:
```python
import math

import jax
import jax.numpy as jnp
from jax import lax
from jax.sharding import PartitionSpec as P

HEADS = 12


EPSILON = 1e-05
THETA = 160000.0
MASKED = -1e30


def layer_norm(values, gain):
    centred = values - jnp.mean(values, axis=-1, keepdims=True)
    spread = jnp.mean(centred * centred, axis=-1, keepdims=True)
    return centred * lax.rsqrt(spread + EPSILON) * gain


def rotary(heads_in, positions):
    half_dim = heads_in.shape[-1] // 2
    counter = jnp.arange(half_dim, dtype=jnp.float32)
    inverse = jnp.exp(counter * (-2.0 * math.log(THETA) / heads_in.shape[-1]))
    angles = positions.astype(jnp.float32)[:, None] * inverse[None, :]
    cosine = jnp.cos(angles)[:, None, :]
    sine_part = jnp.sin(angles)[:, None, :]
    first_half = heads_in[..., :half_dim]
    second = heads_in[..., half_dim:]
    return jnp.concatenate(
        [first_half * cosine - second * sine_part, second * cosine + first_half * sine_part],
        axis=-1,
    )


def geglu(projected):
    half_width = projected.shape[-1] // 2
    inner_part = projected[:, :half_width]
    gating = projected[:, half_width:]
    return 0.5 * inner_part * (1.0 + lax.erf(inner_part * 0.5**0.5)) * gating


def shards(tokens, key_mask, w_qkv, w_attn_out, w_in, w_out, attn_gain, mlp_gain, cotangent):
    seq_here, row_count, width_all = tokens.shape
    head_count = HEADS
    head_width = width_all // head_count
    scaling = head_width ** (-0.5)
    seq_len = row_count * lax.axis_size("ctx")
    block_len = math.gcd(seq_len, 1024)
    num_blocks = seq_len // block_len
    all_rows = seq_here * row_count
    per_head = (all_rows, head_count, head_width)

    def heads_first(rows):
        return jnp.transpose(
            rows.reshape(seq_here, row_count, head_count, head_width), (0, 2, 1, 3)
        )

    def heads_last(rows):
        return jnp.transpose(
            rows.reshape(seq_here, row_count, head_count, head_width), (0, 2, 3, 1)
        )

    def rows_from_first(stacked):
        return jnp.transpose(stacked, (0, 2, 1, 3)).reshape(per_head)

    def rows_from_last(stacked):
        return jnp.transpose(stacked, (0, 3, 1, 2)).reshape(per_head)

    full_qkv, full_attn, full_in, full_out, gain_one, gain_two = (
        lax.all_gather(w_qkv, "wsh", axis=0, tiled=True),
        lax.all_gather(w_attn_out, "wsh", axis=0, tiled=True),
        lax.all_gather(w_in, "wsh", axis=0, tiled=True),
        lax.all_gather(w_out, "wsh", axis=0, tiled=True),
        lax.all_gather(attn_gain, "wsh", axis=0, tiled=True),
        lax.all_gather(mlp_gain, "wsh", axis=0, tiled=True),
    )
    residual_in = tokens.reshape(all_rows, width_all).astype(jnp.float32)
    local_pos = lax.axis_index("ctx") * row_count + jnp.arange(row_count, dtype=jnp.int32)
    positions = jnp.tile(local_pos, seq_here)
    normed_f, norm_one_pull = jax.vjp(layer_norm, residual_in, gain_one.astype(jnp.float32))
    normed = normed_f.astype(jnp.bfloat16)
    joined_proj = jnp.dot(normed, full_qkv, preferred_element_type=jnp.float32)

    def rotate_pair(query_part, key_part):
        return (
            rotary(query_part.reshape(per_head), positions),
            rotary(key_part.reshape(per_head), positions),
        )

    (query_f, key_f), rotate_pull = jax.vjp(
        rotate_pair, joined_proj[:, :width_all], joined_proj[:, width_all : 2 * width_all]
    )
    query_rows_low = query_f.astype(jnp.bfloat16)
    queries = heads_first(query_rows_low)
    keys_own = heads_last(key_f.astype(jnp.bfloat16))
    values_own = heads_last(joined_proj[:, 2 * width_all :].astype(jnp.bfloat16))
    mask_own = key_mask.astype(jnp.bfloat16).reshape(seq_here, 1, 1, row_count)
    keys_all, values_all, mask_all = (
        lax.all_gather(keys_own, "ctx", axis=3, tiled=True),
        lax.all_gather(values_own, "ctx", axis=3, tiled=True),
        lax.all_gather(mask_own, "ctx", axis=3, tiled=True),
    )

    def remote_block(index):
        start = index * block_len
        return (
            lax.dynamic_slice_in_dim(keys_all, start, block_len, 3),
            lax.dynamic_slice_in_dim(values_all, start, block_len, 3),
            lax.dynamic_slice_in_dim(mask_all, start, block_len, 3),
        )

    def forward_step(carried, index):
        running_top, running_total, running_sum = carried
        key_block, value_block, mask_block = remote_block(index)
        raw_scores = (
            jnp.einsum("bhqd,bhdk->bhqk", queries, key_block, preferred_element_type=jnp.float32)
            * scaling
        )
        scores = jnp.where(mask_block > 0.5, raw_scores, MASKED)
        new_top = jnp.maximum(running_top, jnp.max(scores, axis=-1))
        fade_factor = jnp.exp(running_top - new_top)
        weights = jnp.exp(scores - new_top[..., None])
        running_total = running_total * fade_factor + jnp.sum(weights, axis=-1)
        running_sum = running_sum * fade_factor[..., None] + jnp.einsum(
            "bhqk,bhdk->bhqd",
            weights.astype(jnp.bfloat16),
            value_block,
            preferred_element_type=jnp.float32,
        )
        return ((new_top, running_total, running_sum), None)

    stat_shape = (seq_here, head_count, row_count)
    block_ids = jnp.arange(num_blocks, dtype=jnp.int32)
    start_state = (
        jnp.full(stat_shape, MASKED, jnp.float32),
        jnp.zeros(stat_shape, jnp.float32),
        jnp.zeros(stat_shape + (head_width,), jnp.float32),
    )
    (final_top, final_total, final_sum), unused_out = lax.scan(forward_step, start_state, block_ids)
    log_total = final_top + jnp.log(final_total)
    attended_heads = final_sum / final_total[..., None]
    attended = rows_from_first(attended_heads).reshape(all_rows, width_all).astype(jnp.bfloat16)
    hidden = residual_in + jnp.dot(attended, full_attn, preferred_element_type=jnp.float32)
    normed_two_f, norm_two_pull = jax.vjp(layer_norm, hidden, gain_two.astype(jnp.float32))
    normed_two = normed_two_f.astype(jnp.bfloat16)
    projected = jnp.dot(normed_two, full_in, preferred_element_type=jnp.float32)
    gated_f, glu_pull = jax.vjp(geglu, projected)
    gated = gated_f.astype(jnp.bfloat16)
    result = hidden + jnp.dot(gated, full_out, preferred_element_type=jnp.float32)
    outcome = result.astype(jnp.bfloat16).reshape(seq_here, row_count, width_all)
    grad_out = cotangent.reshape(all_rows, width_all)
    grad_w_out = jnp.dot(gated.T, grad_out, preferred_element_type=jnp.float32)
    grad_gated = jnp.dot(grad_out, full_out.T, preferred_element_type=jnp.float32)
    (grad_proj,) = glu_pull(grad_gated)
    grad_proj_low = grad_proj.astype(jnp.bfloat16)
    grad_w_in = jnp.dot(normed_two.T, grad_proj_low, preferred_element_type=jnp.float32)
    grad_norm_two = jnp.dot(grad_proj_low, full_in.T, preferred_element_type=jnp.float32)
    grad_hidden_ln, grad_gain_two = norm_two_pull(grad_norm_two)
    grad_hidden = grad_out.astype(jnp.float32) + grad_hidden_ln
    grad_branch = grad_hidden.astype(jnp.bfloat16)
    grad_w_attn = jnp.dot(attended.T, grad_branch, preferred_element_type=jnp.float32)
    grad_att_rows = (
        jnp.dot(grad_branch, full_attn.T, preferred_element_type=jnp.float32)
        .astype(jnp.bfloat16)
        .reshape(per_head)
    )
    grad_attended = heads_first(grad_att_rows)
    delta_heads = jnp.sum(grad_attended.astype(jnp.float32) * attended_heads, axis=-1)

    def remote_terms(index):
        key_block, value_block, mask_block = remote_block(index)
        raw_scores = (
            jnp.einsum("bhqd,bhdk->bhqk", queries, key_block, preferred_element_type=jnp.float32)
            * scaling
        )
        scores = jnp.where(mask_block > 0.5, raw_scores, MASKED)
        probability = jnp.exp(scores - log_total[..., None])
        grad_probs = jnp.einsum(
            "bhqd,bhdk->bhqk", grad_attended, value_block, preferred_element_type=jnp.float32
        )
        grad_scores = (probability * (grad_probs - delta_heads[..., None])).astype(jnp.bfloat16)
        grad_query_part = (
            jnp.einsum(
                "bhqk,bhdk->bhqd", grad_scores, key_block, preferred_element_type=jnp.float32
            )
            * scaling
        )
        return (probability, grad_scores, grad_query_part)

    whole_zeros = jnp.zeros((seq_here, head_count, head_width, seq_len), jnp.float32)

    def key_step(carried, index):
        grad_query_acc, key_terms, value_terms = carried
        probability, grad_scores, grad_query_part = remote_terms(index)
        grad_value_block = jnp.einsum(
            "bhqk,bhqd->bhdk",
            probability.astype(jnp.bfloat16),
            grad_attended,
            preferred_element_type=jnp.float32,
        )
        grad_key_block = (
            jnp.einsum("bhqk,bhqd->bhdk", grad_scores, queries, preferred_element_type=jnp.float32)
            * scaling
        )
        start = index * block_len
        key_terms = lax.dynamic_update_slice_in_dim(key_terms, grad_key_block, start, 3)
        value_terms = lax.dynamic_update_slice_in_dim(value_terms, grad_value_block, start, 3)
        return ((grad_query_acc + grad_query_part, key_terms, value_terms), None)

    (grad_query_heads, key_terms, value_terms), unused_steps = lax.scan(
        key_step,
        (jnp.zeros(stat_shape + (head_width,), jnp.float32), whole_zeros, whole_zeros),
        block_ids,
    )
    grad_key_heads, grad_value_heads = (
        lax.psum_scatter(key_terms, "ctx", scatter_dimension=3, tiled=True),
        lax.psum_scatter(value_terms, "ctx", scatter_dimension=3, tiled=True),
    )
    grad_query = rows_from_first(grad_query_heads)
    grad_key = rows_from_last(grad_key_heads)
    grad_value = rows_from_last(grad_value_heads)
    grad_query_pre, grad_key_pre = rotate_pull((grad_query, grad_key))
    grad_joined = jnp.concatenate(
        [grad_query_pre, grad_key_pre, grad_value.reshape(all_rows, width_all)], axis=1
    ).astype(jnp.bfloat16)
    grad_w_qkv = jnp.dot(normed.T, grad_joined, preferred_element_type=jnp.float32)
    grad_normed = jnp.dot(grad_joined, full_qkv.T, preferred_element_type=jnp.float32)
    grad_in_ln, grad_gain_one = norm_one_pull(grad_normed)
    grad_tokens = (
        (grad_hidden + grad_in_ln).astype(jnp.bfloat16).reshape(seq_here, row_count, width_all)
    )
    every_part = (
        lax.psum_scatter(
            grad_w_qkv.astype(jnp.bfloat16), "wsh", scatter_dimension=0, tiled=True
        ).astype(jnp.float32),
        lax.psum_scatter(
            grad_w_attn.astype(jnp.bfloat16), "wsh", scatter_dimension=0, tiled=True
        ).astype(jnp.float32),
        lax.psum_scatter(
            grad_w_in.astype(jnp.bfloat16), "wsh", scatter_dimension=0, tiled=True
        ).astype(jnp.float32),
        lax.psum_scatter(
            grad_w_out.astype(jnp.bfloat16), "wsh", scatter_dimension=0, tiled=True
        ).astype(jnp.float32),
        lax.psum_scatter(
            grad_gain_one.astype(jnp.bfloat16), "wsh", scatter_dimension=0, tiled=True
        ).astype(jnp.float32),
        lax.psum_scatter(
            grad_gain_two.astype(jnp.bfloat16), "wsh", scatter_dimension=0, tiled=True
        ).astype(jnp.float32),
    )
    sum_qkv, sum_attn, sum_in, sum_out, sum_gain_one, sum_gain_two = lax.psum(
        (every_part[0], every_part[1], every_part[2], every_part[3], every_part[4], every_part[5]),
        "ctx",
    )
    return (outcome, grad_tokens, sum_gain_one, sum_gain_two, sum_qkv, sum_attn, sum_in, sum_out)


def solution(mesh):
    return jax.shard_map(
        shards,
        mesh=mesh,
        in_specs=(
            P("wsh", "ctx", None),
            P("wsh", "ctx"),
            P("wsh", None),
            P("wsh", None),
            P("wsh", None),
            P("wsh", None),
            P("wsh"),
            P("wsh"),
            P("wsh", "ctx", None),
        ),
        out_specs=(
            P("wsh", "ctx", None),
            P("wsh", "ctx", None),
            P("wsh"),
            P("wsh"),
            P("wsh", None),
            P("wsh", None),
            P("wsh", None),
            P("wsh", None),
        ),
        check_vma=False,
    )
```

profile of v0, /device:TPU:17, one launch (start us, length us, event | category | flops | bytes accessed | tf_op | source)
XLA Modules:
  0.0 766.7 jit_solution(94271806940288713)
XLA Ops:
  7.2 0.7 all-gather.8.cloned.1.call-update
  8.0 1.3 fusion.53
  10.0 0.8 dynamic-update-slice
  10.8 0.8 dynamic-update-slice.1
  11.6 7.0 all-reduce.12
  18.6 1.2 convert_reduce_fusion
  19.8 1.3 multiply_reduce_fusion.6
  21.1 0.8 multiply_cosine_fusion
  22.0 1.2 multiply_convert_fusion.3
  23.2 56.2 %all-gather.8.cloned.1.call-done = bf16[768,2304]{1,0:T(8,128)(2,1)} async-done(((bf16[192,2304]{1,0:T(8,128)(2,1)}), bf16[768,2304]{1,0:T(8,128)(2,1)}) %all-gather.8.cloned.1.call-update) | async-done | bytes 3538960 | tf_op jit(solution)/shard_map/all_gather | solution.py:72
  79.4 3.1 fusion.55
  82.5 1.2 fusion.52
  83.7 1.4 copy.32
  85.1 2.3 copy.35
  87.4 1.4 fusion.30
  88.9 0.8 maximum_bitcast_fusion.1
  90.1 0.8 copy.83
  91.0 0.5 all-gather.14.cloned.1.call-update
  91.6 0.5 all-gather.16.cloned.1.call-update
  92.2 0.5 all-gather.18.cloned.1.call-update
  92.8 9.2 %all-gather = bf16[2,1024]{1,0:T(2,128)(2,1)S(1)} all-gather(bf16[2,128]{1,0:T(2,128)(2,1)S(1)} %convert_element_type.123), channel_id=2, replica_groups=mesh['ctx'=8,'wsh'=4] {'ctx'}, dimensions={1}, use_global_device_ids=true | all-gather | bytes 4608 | tf_op jit(solution)/shard_map/all_gather | solution.py:103
  102.0 21.0 %all-gather.10.cloned.1.call-done = bf16[2,12,64,1024]{3,2,1,0:T(8,128)(2,1)} async-done(((bf16[2,12,64,128]{3,2,1,0:T(8,128)(2,1)}), bf16[2,12,64,1024]{3,2,1,0:T(8,128)(2,1)}) %all-gather.10.cloned.1.call-update) | async-done | bytes 3145744 | tf_op jit(solution)/shard_map/all_gather | solution.py:101
  123.1 3.9 fusion.3
  127.0 3.3 fusion
  130.3 1.2 copy-done
  131.5 0.6 exponential_multiply_fusion
  132.1 26.2 %all-gather.12.cloned.1.call-done = bf16[2,12,64,1024]{3,2,1,0:T(8,128)(2,1)} async-done(((bf16[2,12,64,128]{3,2,1,0:T(8,128)(2,1)}), bf16[2,12,64,1024]{3,2,1,0:T(8,128)(2,1)}) %all-gather.12.cloned.1.call-update) | async-done | bytes 3145744 | tf_op jit(solution)/shard_map/all_gather | solution.py:102
  158.4 9.3 %fusion.17 = (bf16[2,128,12,64]{1,3,2,0:T(8,128)(2,1)S(1)}, f32[2,12,128,64]{2,3,1,0:T(8,128)}) fusion(f32[2,128,12]{1,2,0:T(8,128)S(1)} %bitcast_add_fusion.1, f32[2,128,12]{1,2,0:T(8,128)S(1)} %get-tuple-element.101, bf16[2,12,64,1024]{3,2,1,0:T(8,128)(2,1)} %all-gather.12.cloned.1.call-done, f32[2,12,128,1024]{3,2,1,0:T(8,128)} %copy-done, ...), kind=kOutput, calls=%fused_computation.41 | convolution fusion | flops 415825920 | bytes 16947200 | tf_op jit(solution)/shard_map/while/body/eval_jaxpr/bhqk,bhdk->bhqd/dot_general | solution.py:126
  168.1 20.9 %all-gather.14.cloned.1.call-done = bf16[768,768]{1,0:T(8,128)(2,1)} async-done(((bf16[192,768]{1,0:T(8,128)(2,1)}), bf16[768,768]{1,0:T(8,128)(2,1)}) %all-gather.14.cloned.1.call-update) | async-done | bytes 1179664 | tf_op jit(solution)/shard_map/all_gather | solution.py:73
  189.0 1.9 fusion.54
  191.1 67.9 %all-gather.16.cloned.1.call-done = bf16[768,2304]{1,0:T(8,128)(2,1)} async-done(((bf16[192,2304]{1,0:T(8,128)(2,1)}), bf16[768,2304]{1,0:T(8,128)(2,1)}) %all-gather.16.cloned.1.call-update) | async-done | bytes 3538960 | tf_op jit(solution)/shard_map/all_gather | solution.py:74
  259.0 4.6 fusion.50
  263.6 36.1 %all-gather.18.cloned.1.call-done = bf16[1152,768]{1,0:T(8,128)(2,1)} async-done(((bf16[288,768]{1,0:T(8,128)(2,1)}), bf16[1152,768]{1,0:T(8,128)(2,1)}) %all-gather.18.cloned.1.call-update) | async-done | bytes 1769488 | tf_op jit(solution)/shard_map/all_gather | solution.py:75
  299.6 4.1 fusion.24
  303.8 1.8 multiply_reduce_fusion
  305.9 0.6 copy-done.27
  307.3 0.9 copy.41
  308.3 1.1 reshape_reshape.8
  309.4 10.2 %fusion.4 = f32[2,12,64,1024]{3,2,1,0:T(8,128)} fusion(f32[2,12,128,1024]{3,2,1,0:T(8,128)} %copy-done, f32[2,12,128]{2,1,0:T(8,128)} %get-tuple-element.102, pred[2,1024]{1,0:T(4,128)(4,1)S(1)} %broadcast_compare_fusion, bf16[2,128,12,64]{1,0,3,2:T(2,128)(2,1)S(1)} %reshape_reshape.8), kind=kOutput, calls=%fused_computation.8 | convolution fusion | flops 415236096 | bytes 19281920 | tf_op jit(solution)/shard_map/while/body/eval_jaxpr/bhqk,bhqd->bhdk/dot_general | solution.py:197
  319.6 1.4 multiply_reduce_fusion.3
  321.0 8.5 %multiply_convert_fusion = bf16[2,12,128,1024]{3,2,1,0:T(8,128)(2,1)S(1)} fusion(f32[2,12,128,1024]{3,2,1,0:T(8,128)} %copy-done, f32[2,12,128]{2,1,0:T(8,128)S(1)} %multiply_reduce_fusion.3, f32[2,12,128]{2,1,0:T(8,128)} %get-tuple-element.102, pred[2,1024]{1,0:T(4,128)(4,1)S(1)} %broadcast_compare_fusion, ...), kind=kOutput, calls=%fused_computation | convolution fusion | flops 421527552 | bytes 22439936 | tf_op jit(solution)/shard_map/while/body/eval_jaxpr/bhqd,bhdk->bhqk/dot_general | solution.py:180
  329.5 3.1 copy-done.1
  332.6 3.7 broadcast_multiply_fusion
  336.4 1.5 convolution_convert_fusion.3
  338.0 3.0 convolution_convert_fusion.2
  341.0 4.7 convolution_convert_fusion
  345.8 6.0 fusion.13
  351.8 29.7 %reduce-scatter.9.cloned.1.call-done = f32[2,12,64,128]{3,2,1,0:T(8,128)} async-done(((f32[2,12,64,1024]{3,2,1,0:T(8,128)}), f32[2,12,64,128]{3,2,1,0:T(8,128)}) %reduce-scatter.9.cloned.1.call-update) | async-done | bytes 786448 | tf_op jit(solution)/shard_map/reduce_scatter | solution.py:219
  381.5 1.2 convert_bitcast_fusion
  383.1 0.8 copy.82
  383.9 63.1 %reduce-scatter.7.cloned.1.call-done = f32[2,12,64,128]{3,2,1,0:T(8,128)} async-done(((f32[2,12,64,1024]{3,2,1,0:T(8,128)}), f32[2,12,64,128]{3,2,1,0:T(8,128)}) %reduce-scatter.7.cloned.1.call-update) | async-done | bytes 786448 | tf_op jit(solution)/shard_map/reduce_scatter | solution.py:218
  447.0 1.2 copy_bitcast_fusion
  448.2 1.1 multiply_add_fusion.4
  449.5 0.7 copy-done.18
  450.3 2.9 convolution_convert_fusion.1
  454.3 2.9 fusion.14
  457.2 20.7 %reduce-scatter.13.cloned.1.call-done = bf16[192,768]{1,0:T(8,128)(2,1)} async-done(((bf16[768,768]{1,0:T(8,128)(2,1)}), bf16[192,768]{1,0:T(8,128)(2,1)}) %reduce-scatter.13.cloned.1.call-update) | async-done | bytes 294928 | tf_op jit(solution)/shard_map/reduce_scatter | solution.py:238
  477.9 40.3 %reduce-scatter.17.cloned.1.call-done = bf16[288,768]{1,0:T(8,128)(2,1)} async-done(((bf16[1152,768]{1,0:T(8,128)(2,1)}), bf16[288,768]{1,0:T(8,128)(2,1)}) %reduce-scatter.17.cloned.1.call-update) | async-done | bytes 442384 | tf_op jit(solution)/shard_map/reduce_scatter | solution.py:244
  518.2 69.1 %reduce-scatter.15.cloned.1.call-done = bf16[192,2304]{1,0:T(8,128)(2,1)} async-done(((bf16[768,2304]{1,0:T(8,128)(2,1)}), bf16[192,2304]{1,0:T(8,128)(2,1)}) %reduce-scatter.15.cloned.1.call-update) | async-done | bytes 884752 | tf_op jit(solution)/shard_map/reduce_scatter | solution.py:241
  587.3 3.5 multiply_reduce_fusion.2
  591.2 6.5 all-reduce.11
  597.9 1.1 add_convert_fusion.1
  599.0 57.3 %reduce-scatter.11.cloned.1.call-done = bf16[192,2304]{1,0:T(8,128)(2,1)} async-done(((bf16[768,2304]{1,0:T(8,128)(2,1)}), bf16[192,2304]{1,0:T(8,128)(2,1)}) %reduce-scatter.11.cloned.1.call-update) | async-done | bytes 884752 | tf_op jit(solution)/shard_map/reduce_scatter | solution.py:235
  656.3 103.6 %all-reduce.14 = (f32[192]{0:T(256)}, f32[192]{0:T(256)}, f32[192,2304]{1,0:T(8,128)}, f32[192,768]{1,0:T(8,128)}, f32[192,2304]{1,0:T(8,128)}, /*index=5*/f32[288,768]{1,0:T(8,128)}) all-reduce(f32[192]{0:T(256)S(1)} %dynamic-slice_convert_fusion.1, ...), channel_id=1, replica_groups=mesh['ctx'=8,'wsh'=4] {'ctx'}, use_global_device_ids=true, to_apply=%region_15.16 | all-reduce | flops 1253760 | bytes 7523328 | tf_op jit(solution)/shard_map/psum | solution.py:254
  (118 shorter events, 4.8 us)
Async XLA Ops:
  7.2 72.2 %all-gather.8.cloned.1.call-start = ((), (), s32[]{:S(2)}) async-start(), calls=%async_computation.6 | async-start | bytes 4423680 | tf_op jit(solution)/shard_map/all_gather | solution.py:72
  7.9 115.2 %all-gather.10.cloned.1.call-start = ((), (), s32[]{:S(2)}) async-start(), calls=%async_computation.7 | async-start | bytes 3538944 | tf_op jit(solution)/shard_map/all_gather | solution.py:101
  19.8 62.6 %copy-start.23 = (f32[256]{0:T(256)}, f32[256]{0:T(256)S(1)}, u32[]{:S(2)}) copy-start(f32[256]{0:T(256)S(1)} %get-tuple-element.106) | copy-start | bytes 3076
  21.1 61.4 %copy-start.29 = (f32[2,128]{1,0:T(2,128)}, f32[2,128]{1,0:T(2,128)S(1)}, u32[]{:S(2)}) copy-start(f32[2,128]{1,0:T(2,128)S(1)} %multiply_reduce_fusion.6) | copy-start | bytes 3076
  21.1 61.4 %copy-start.25 = (f32[256]{0:T(256)}, f32[256]{0:T(256)S(1)}, u32[]{:S(2)}) copy-start(f32[256]{0:T(256)S(1)} %bitcast_rsqrt_fusion) | copy-start | bytes 3076
  23.2 59.3 %copy-start.11 = (bf16[256,768]{1,0:T(8,128)(2,1)}, bf16[256,768]{1,0:T(8,128)(2,1)S(1)}, u32[]{:S(2)}) copy-start(bf16[256,768]{1,0:T(8,128)(2,1)S(1)} %multiply_convert_fusion.3) | copy-start | bytes 1179652
  88.9 3.9 copy-start.32
  89.7 68.6 %all-gather.12.cloned.1.call-start = ((), (), s32[]{:S(2)}) async-start(), calls=%async_computation.8 | async-start | bytes 3538944 | tf_op jit(solution)/shard_map/all_gather | solution.py:102
  90.9 98.0 %all-gather.14.cloned.1.call-start = ((), (), s32[]{:S(2)}) async-start(), calls=%async_computation.9 | async-start | bytes 1474560 | tf_op jit(solution)/shard_map/all_gather | solution.py:73
  91.5 167.5 %all-gather.16.cloned.1.call-start = ((), (), s32[]{:S(2)}) async-start(), calls=%async_computation.10 | async-start | bytes 4423680 | tf_op jit(solution)/shard_map/all_gather | solution.py:74
  92.1 207.5 %all-gather.18.cloned.1.call-start = ((), (), s32[]{:S(2)}) async-start(), calls=%async_computation.11 | async-start | bytes 2211840 | tf_op jit(solution)/shard_map/all_gather | solution.py:75
  92.7 288.8 %reduce-scatter.9.cloned.1.call-start = ((), (), s32[]{:S(2)}) async-start(), calls=%async_computation.13 | async-start | bytes 7077888 | tf_op jit(solution)/shard_map/reduce_scatter | solution.py:219
  102.0 24.9 %copy-start.7 = (bf16[2,128,12,32]{1,3,2,0:T(8,128)(2,1)}, bf16[2,128,12,32]{1,3,2,0:T(8,128)(2,1)S(1)}, u32[]{:S(2)}) copy-start(bf16[2,128,12,32]{1,3,2,0:T(8,128)(2,1)S(1)} %get-tuple-element.121) | copy-start | bytes 589828
  102.0 24.9 %copy-start.9 = (bf16[2,128,12,32]{1,3,2,0:T(8,128)(2,1)}, bf16[2,128,12,32]{1,3,2,0:T(8,128)(2,1)S(1)}, u32[]{:S(2)}) copy-start(bf16[2,128,12,32]{1,3,2,0:T(8,128)(2,1)S(1)} %get-tuple-element.122) | copy-start | bytes 589828
  127.0 4.5 copy-start
  158.4 30.6 %copy-start.2 = (bf16[2,128,768]{2,1,0:T(8,128)(2,1)S(1)}, bf16[2,128,768]{2,1,0:T(8,128)(2,1)}, u32[]{:S(2)}) copy-start(bf16[2,128,768]{2,1,0:T(8,128)(2,1)} %param.9) | copy-start | bytes 1179652
  191.1 114.5 %copy-start.21 = (f32[256]{0:T(256)}, f32[256]{0:T(256)S(1)}, u32[]{:S(2)}) copy-start(f32[256]{0:T(256)S(1)} %fusion.35) | copy-start | bytes 3076
  191.1 108.6 %copy-start.5 = (bf16[2,128,768]{2,1,0:T(8,128)(2,1)S(1)}, bf16[2,128,768]{2,1,0:T(8,128)(2,1)}, u32[]{:S(2)}) copy-start(bf16[2,128,768]{2,1,0:T(8,128)(2,1)} %param.17) | copy-start | bytes 1179652
  299.6 4.1 copy-start.4
  303.8 1.8 copy-start.13
  303.8 1.8 copy-start.14
  305.6 1.3 copy-start.3
  305.9 0.6 copy-start.27
  319.6 127.4 %reduce-scatter.7.cloned.1.call-start = ((), (), s32[]{:S(2)}) async-start(), calls=%async_computation.12 | async-start | bytes 7077888 | tf_op jit(solution)/shard_map/reduce_scatter | solution.py:218
  321.0 11.6 %copy-start.8 = (bf16[2,128,12,32]{1,3,2,0:T(8,128)(2,1)S(1)}, bf16[2,128,12,32]{1,3,2,0:T(8,128)(2,1)}, u32[]{:S(2)}) copy-start(bf16[2,128,12,32]{1,3,2,0:T(8,128)(2,1)} %copy-done.7) | copy-start | bytes 589828
  321.0 11.6 %copy-start.10 = (bf16[2,128,12,32]{1,3,2,0:T(8,128)(2,1)S(1)}, bf16[2,128,12,32]{1,3,2,0:T(8,128)(2,1)}, u32[]{:S(2)}) copy-start(bf16[2,128,12,32]{1,3,2,0:T(8,128)(2,1)} %copy-done.9) | copy-start | bytes 589828
  329.5 3.1 copy-start.1
  336.4 141.5 %reduce-scatter.13.cloned.1.call-start = ((), (), s32[]{:S(2)}) async-start(), calls=%async_computation.15 | async-start | bytes 1474560 | tf_op jit(solution)/shard_map/reduce_scatter | solution.py:238
  337.9 3.1 copy-start.22
  337.9 180.2 %reduce-scatter.17.cloned.1.call-start = ((), (), s32[]{:S(2)}) async-start(), calls=%async_computation.17 | async-start | bytes 2211840 | tf_op jit(solution)/shard_map/reduce_scatter | solution.py:244
  341.0 246.3 %reduce-scatter.15.cloned.1.call-start = ((), (), s32[]{:S(2)}) async-start(), calls=%async_computation.16 | async-start | bytes 4423680 | tf_op jit(solution)/shard_map/reduce_scatter | solution.py:241
  345.7 310.6 %reduce-scatter.11.cloned.1.call-start = ((), (), s32[]{:S(2)}) async-start(), calls=%async_computation.14 | async-start | bytes 4423680 | tf_op jit(solution)/shard_map/reduce_scatter | solution.py:235
  448.2 2.1 copy-start.12
  448.2 2.1 copy-start.16
  449.4 0.7 copy-start.18
  449.5 0.8 copy-start.19
  453.2 1.1 copy-start.6
  453.2 134.1 %copy-start.17 = (bf16[96,8,2,128]{3,1,2,0:T(8,128)(2,1)S(1)}, bf16[96,8,2,128]{3,1,2,0:T(8,128)(2,1)}, u32[]{:S(2)}) copy-start(bf16[96,8,2,128]{3,1,2,0:T(8,128)(2,1)} %copy.82) | copy-start | bytes 1179652
  453.2 134.1 %copy-start.24 = (f32[256]{0:T(256)S(1)}, f32[256]{0:T(256)}, u32[]{:S(2)}) copy-start(f32[256]{0:T(256)} %copy-done.23) | copy-start | bytes 3076
  457.2 133.6 %copy-start.30 = (f32[2,128]{1,0:T(2,128)S(1)}, f32[2,128]{1,0:T(2,128)}, u32[]{:S(2)}) copy-start(f32[2,128]{1,0:T(2,128)} %copy-done.29) | copy-start | bytes 3076
  457.2 133.6 %copy-start.26 = (f32[256]{0:T(256)S(1)}, f32[256]{0:T(256)}, u32[]{:S(2)}) copy-start(f32[256]{0:T(256)} %copy-done.25) | copy-start | bytes 3076
  457.2 134.0 %copy-start.31 = (bf16[768]{0:T(1024)(128)(2,1)S(1)}, bf16[768]{0:T(1024)(128)(2,1)}, u32[]{:S(2)}) copy-start(bf16[768]{0:T(1024)(128)(2,1)} %get-tuple-element.54) | copy-start | bytes 4612
  457.2 140.7 %copy-start.28 = (f32[256]{0:T(256)S(1)}, f32[256]{0:T(256)}, u32[]{:S(2)}) copy-start(f32[256]{0:T(256)} %copy-done.27) | copy-start | bytes 3076
  590.7 65.6 %copy-start.15 = (bf16[288,768]{1,0:T(8,128)(2,1)S(1)}, bf16[288,768]{1,0:T(8,128)(2,1)}, u32[]{:S(2)}) copy-start(bf16[288,768]{1,0:T(8,128)(2,1)} %reduce-scatter.17.cloned.1.call-done) | copy-start | bytes 1327108
  590.8 65.6 %copy-start.20 = (bf16[192,768]{1,0:T(8,128)(2,1)S(1)}, bf16[192,768]{1,0:T(8,128)(2,1)}, u32[]{:S(2)}) copy-start(bf16[192,768]{1,0:T(8,128)(2,1)} %reduce-scatter.13.cloned.1.call-done) | copy-start | bytes 884740
Sparse Core Ops, SparseCore 0:
  9.6 69.7 all-gather.7
  89.8 33.1 all-gather.9
  125.5 32.8 all-gather.11
  159.8 29.1 all-gather.13
  190.4 68.5 all-gather.15
  260.4 39.1 all-gather.17
  319.7 61.7 reduce-scatter.8
  385.2 61.7 reduce-scatter.6
  449.9 27.9 reduce-scatter.12
  480.6 37.4 reduce-scatter.16
  520.6 66.6 reduce-scatter.14
  589.5 66.7 reduce-scatter.10
where the time goes:
time: 770 us; the launch traced here: 767 us
  waiting for transfers between devices  511 us (66%)
  blocking collectives  126 us (16%)
  matrix products  75.9 us (10%)
  local copies, waits for them, and re-layouts  20.4 us (3%)
  other arithmetic  16.8 us (2%)
  between operations  16.1 us (2%)
    psum x1, blocking collectives, shards(): lax.psum((every_part[0], every_part[1], every_part[2], every_part[3], eve...  104 us
    reduce_scatter x1, waiting for transfers between devices, shards(): lax.psum_scatter(grad_w_in.astype(jnp.bfloat16), 'wsh', scatter_dimension...  69.1 us
    all_gather x1, waiting for transfers between devices, shards(): lax.all_gather(w_in, 'wsh', axis=0, tiled=True)  67.9 us
    reduce_scatter x1, waiting for transfers between devices, shards(): lax.psum_scatter(key_terms, 'ctx', scatter_dimension=3, tiled=True)  63.1 us
    reduce_scatter x1, waiting for transfers between devices, shards(): lax.psum_scatter(grad_w_qkv.astype(jnp.bfloat16), 'wsh', scatter_dimensio...  57.3 us
    all_gather x1, waiting for transfers between devices, shards(): lax.all_gather(w_qkv, 'wsh', axis=0, tiled=True)  56.2 us
    reduce_scatter x1, waiting for transfers between devices, shards(): lax.psum_scatter(grad_w_out.astype(jnp.bfloat16), 'wsh', scatter_dimensio...  40.3 us
    all_gather x1, waiting for transfers between devices, shards(): lax.all_gather(w_out, 'wsh', axis=0, tiled=True)  36.1 us
  transfers between devices with their start and end apart: 12, of which 12 were waited for; matrix products, arithmetic and copies ran while one was open for 10% of the time, Pallas kernels for 0%

commit v1 on v0

--- a/solution.py
+++ b/solution.py
@@ -3,6 +3,8 @@
 import jax
 import jax.numpy as jnp
 from jax import lax
+from jax.experimental import pallas as pl
+from jax.experimental.pallas import tpu as pltpu
 from jax.sharding import PartitionSpec as P
 
 HEADS = 12
@@ -41,7 +43,7 @@
     return 0.5 * inner_part * (1.0 + lax.erf(inner_part * 0.5**0.5)) * gating
 
 
-def shards(tokens, key_mask, w_qkv, w_attn_out, w_in, w_out, attn_gain, mlp_gain, cotangent):
+def by_positions(tokens, key_mask, w_qkv, w_attn_out, w_in, w_out, attn_gain, mlp_gain, cotangent):
     seq_here, row_count, width_all = tokens.shape
     head_count = HEADS
     head_width = width_all // head_count
@@ -258,6 +260,232 @@
     return (outcome, grad_tokens, sum_gain_one, sum_gain_two, sum_qkv, sum_attn, sum_in, sum_out)
 
 
+NT = (((1,), (1,)), ((), ()))
+NN = (((1,), (0,)), ((), ()))
+TN = (((0,), (0,)), ((), ()))
+
+
+def mm(left, right, dims=NN):
+    return lax.dot_general(left, right, dims, preferred_element_type=jnp.float32)
+
+
+def attend_kernel(q_ref, k_ref, v_ref, mask_ref, o_ref, p_ref):
+    width = q_ref.shape[1]
+    scores = mm(k_ref[0], q_ref[0], TN) * width ** (-0.5)
+    scores = jnp.where(mask_ref[...] > 0.5, scores, MASKED)
+    top = jnp.max(scores, axis=0, keepdims=True)
+    weights = jnp.exp(scores - top)
+    prob = weights * (1.0 / jnp.sum(weights, axis=0, keepdims=True))
+    p_ref[0] = prob
+    o_ref[0] = mm(v_ref[0], prob.astype(jnp.bfloat16))
+
+
+def attend(queries, keys, values, mask_col):
+    pairs, width, length = queries.shape
+    rows = math.gcd(length, 256)
+    one = lambda: pl.BlockSpec((1, width, length), lambda i, j: (i, 0, 0))
+    part = lambda: pl.BlockSpec((1, width, rows), lambda i, j: (i, 0, j))
+    return pl.pallas_call(
+        attend_kernel,
+        grid=(pairs, length // rows),
+        in_specs=[part(), one(), one(), pl.BlockSpec((length, 1), lambda i, j: (0, 0))],
+        out_specs=[part(), pl.BlockSpec((1, length, rows), lambda i, j: (i, 0, j))],
+        out_shape=[
+            jax.ShapeDtypeStruct((pairs, width, length), jnp.float32),
+            jax.ShapeDtypeStruct((pairs, length, length), jnp.float32),
+        ],
+        compiler_params=pltpu.CompilerParams(vmem_limit_bytes=40 * 2**20),
+        cost_estimate=pl.CostEstimate(
+            flops=4 * pairs * width * length**2,
+            bytes_accessed=4 * pairs * length**2,
+            transcendentals=pairs * length**2,
+        ),
+    )(queries, keys, values, mask_col)
+
+
+def attend_back_kernel(q_ref, k_ref, v_ref, do_ref, o_ref, p_ref, dq_ref, dk_ref, dv_ref):
+    step = pl.program_id(1)
+    scaling = q_ref.shape[1] ** (-0.5)
+    grad_out = do_ref[0]
+    delta = jnp.sum(grad_out.astype(jnp.float32) * o_ref[0], axis=0, keepdims=True)
+    prob = p_ref[0]
+    grad_prob = mm(v_ref[0], grad_out, TN)
+    grad_scores = (prob * (grad_prob - delta)).astype(jnp.bfloat16)
+    dq_ref[0] = mm(k_ref[0], grad_scores) * scaling
+
+    @pl.when(step == 0)
+    def _():
+        dk_ref[...] = jnp.zeros_like(dk_ref)
+        dv_ref[...] = jnp.zeros_like(dv_ref)
+
+    dk_ref[0] += mm(q_ref[0], grad_scores, NT) * scaling
+    dv_ref[0] += mm(grad_out, prob.astype(jnp.bfloat16), NT)
+
+
+def attend_back(queries, keys, values, grad_out, mixed, prob):
+    pairs, width, length = queries.shape
+    rows = math.gcd(length, 256)
+    one = lambda: pl.BlockSpec((1, width, length), lambda i, j: (i, 0, 0))
+    part = lambda: pl.BlockSpec((1, width, rows), lambda i, j: (i, 0, j))
+    shape = jax.ShapeDtypeStruct((pairs, width, length), jnp.float32)
+    return pl.pallas_call(
+        attend_back_kernel,
+        grid=(pairs, length // rows),
+        in_specs=[
+            part(),
+            one(),
+            one(),
+            part(),
+            part(),
+            pl.BlockSpec((1, length, rows), lambda i, j: (i, 0, j)),
+        ],
+        out_specs=[part(), one(), one()],
+        out_shape=[shape, shape, shape],
+        compiler_params=pltpu.CompilerParams(vmem_limit_bytes=40 * 2**20),
+        cost_estimate=pl.CostEstimate(
+            flops=8 * pairs * width * length**2,
+            bytes_accessed=4 * pairs * length**2,
+            transcendentals=0,
+        ),
+    )(queries, keys, values, grad_out, mixed, prob)
+
+
+def gather_rows(part):
+    pieces = lax.axis_size("ctx")
+    rows = part.shape[0] // pieces
+    mine = lax.dynamic_slice_in_dim(part, lax.axis_index("ctx") * rows, rows, 0)
+    return lax.all_gather(mine, ("wsh", "ctx"), axis=0, tiled=True)
+
+
+def sum_rows(term):
+    total, width = term.shape
+    fold = 2 if total % 256 else 1
+    term = term.astype(jnp.bfloat16).reshape(total * fold, width // fold)
+    piece = lax.psum_scatter(term, ("wsh", "ctx"), scatter_dimension=0, tiled=True)
+    sums = lax.all_gather(piece, "ctx", axis=0, tiled=True)
+    return sums.reshape(-1, width).astype(jnp.float32)
+
+
+def by_heads(tokens, key_mask, w_qkv, w_attn_out, w_in, w_out, attn_gain, mlp_gain, cotangent):
+    seqs, rows, width = tokens.shape
+    peers = lax.axis_size("ctx")
+    head_width = width // HEADS
+    half = head_width // 2
+    pairs = seqs * HEADS // peers
+    splits = peers // seqs
+    feats = pairs * head_width
+    length = rows * peers
+    tokens_here = seqs * rows
+    low = jnp.bfloat16
+
+    gains = lax.all_gather(jnp.stack([attn_gain, mlp_gain]), "wsh", axis=1, tiled=True)
+    gain_one, gain_two = gains[0], gains[1]
+    full_qkv = gather_rows(w_qkv)
+    full_attn = gather_rows(w_attn_out)
+    full_in = gather_rows(w_in)
+    full_out = gather_rows(w_out)
+
+    def to_heads(parts):
+        count = parts.shape[0]
+        sent = jnp.transpose(
+            parts.reshape(count, splits, feats, seqs, rows), (3, 1, 0, 2, 4)
+        ).reshape(peers, count * feats, rows)
+        return sent
+
+    def swap(sent):
+        return lax.all_to_all(sent, "ctx", split_axis=0, concat_axis=0, tiled=True)
+
+    def to_rows(parts):
+        count = parts.shape[0]
+        sent = jnp.transpose(
+            parts.astype(low).reshape(count * feats, peers, rows), (1, 0, 2)
+        )
+        got = swap(sent).reshape(seqs, splits, count, feats, rows)
+        return jnp.transpose(got, (2, 1, 3, 0, 4)).reshape(count, width, tokens_here)
+
+    residual_in = tokens.reshape(tokens_here, width).astype(jnp.float32)
+    normed_f, norm_one_pull = jax.vjp(layer_norm, residual_in, gain_one.astype(jnp.float32))
+    normed = normed_f.astype(low)
+    joined = mm(full_qkv, normed, (((0,), (1,)), ((), ())))
+
+    local_pos = lax.axis_index("ctx") * rows + jnp.arange(rows, dtype=jnp.int32)
+    inverse = jnp.exp(
+        jnp.arange(half, dtype=jnp.float32) * (-2.0 * math.log(THETA) / head_width)
+    )
+    angles = inverse[:, None] * jnp.tile(local_pos, seqs).astype(jnp.float32)[None, :]
+    cosine, sine = jnp.cos(angles), jnp.sin(angles)
+
+    def turn(values, way):
+        pair = values.reshape(HEADS, 2, half, tokens_here)
+        first, second = pair[:, 0], pair[:, 1]
+        return jnp.stack(
+            [first * cosine - way * (second * sine), second * cosine + way * (first * sine)], axis=1
+        ).reshape(width, tokens_here)
+
+    trio = jnp.stack(
+        [turn(joined[:width], 1.0), turn(joined[width : 2 * width], 1.0), joined[2 * width :]]
+    ).astype(low)
+    mask_rows = jnp.broadcast_to(
+        key_mask.astype(low)[:, None, None, :], (seqs, splits, 16, rows)
+    ).reshape(peers, 16, rows)
+    got = swap(jnp.concatenate([to_heads(trio), mask_rows], axis=1))
+    got = jnp.transpose(got, (1, 0, 2)).reshape(3 * feats + 16, length)
+    queries, keys, values = (
+        got[i * feats : (i + 1) * feats].reshape(pairs, head_width, length) for i in range(3)
+    )
+    mask_col = got[3 * feats].astype(jnp.float32)[:, None]
+    mixed, prob = attend(queries, keys, values, mask_col)
+    attended = jnp.transpose(to_rows(mixed.reshape(1, feats, length))[0])
+
+    hidden = residual_in + mm(attended, full_attn)
+    normed_two_f, norm_two_pull = jax.vjp(layer_norm, hidden, gain_two.astype(jnp.float32))
+    normed_two = normed_two_f.astype(low)
+    projected = mm(normed_two, full_in)
+    gated_f, glu_pull = jax.vjp(geglu, projected)
+    gated = gated_f.astype(low)
+    outcome = (hidden + mm(gated, full_out)).astype(low).reshape(seqs, rows, width)
+    grad_out = cotangent.reshape(tokens_here, width)
+    grad_w_out = sum_rows(mm(gated, grad_out, TN))
+    (grad_proj,) = glu_pull(mm(grad_out, full_out, NT))
+    grad_proj = grad_proj.astype(low)
+    grad_w_in = sum_rows(mm(normed_two, grad_proj, TN))
+    grad_hidden_ln, grad_gain_two = norm_two_pull(mm(grad_proj, full_in, NT))
+    grad_hidden = grad_out.astype(jnp.float32) + grad_hidden_ln
+    grad_branch = grad_hidden.astype(low)
+    grad_w_attn = sum_rows(mm(attended, grad_branch, TN))
+    grad_att = mm(full_attn, grad_branch, NT).astype(low)
+    got_do = swap(to_heads(grad_att[None]))
+    got_do = jnp.transpose(got_do, (1, 0, 2)).reshape(pairs, head_width, length)
+    grads = attend_back(queries, keys, values, got_do, mixed, prob)
+    back = to_rows(jnp.stack([g.reshape(feats, length) for g in grads])).astype(jnp.float32)
+    grad_joined = jnp.concatenate([turn(back[0], -1.0), turn(back[1], -1.0), back[2]]).astype(low)
+    grad_w_qkv = sum_rows(mm(normed, grad_joined, (((0,), (1,)), ((), ()))))
+    grad_normed = mm(grad_joined, full_qkv, (((0,), (1,)), ((), ())))
+    grad_in_ln, grad_gain_one = norm_one_pull(grad_normed)
+    grad_tokens = (grad_hidden + grad_in_ln).astype(low).reshape(seqs, rows, width)
+    gain_sums = lax.psum(jnp.stack([grad_gain_one, grad_gain_two]), ("ctx", "wsh"))
+    share = attn_gain.shape[0]
+    gain_sums = lax.dynamic_slice_in_dim(gain_sums, lax.axis_index("wsh") * share, share, 1)
+    return (
+        outcome,
+        grad_tokens,
+        gain_sums[0],
+        gain_sums[1],
+        grad_w_qkv,
+        grad_w_attn,
+        grad_w_in,
+        grad_w_out,
+    )
+
+
+def shards(*arrays):
+    seqs = arrays[0].shape[0]
+    peers = lax.axis_size("ctx")
+    even = (seqs * HEADS) % peers == 0 and peers % seqs == 0
+    even = even and all(w.shape[0] % peers == 0 for w in arrays[2:6])
+    return (by_heads if even else by_positions)(*arrays)
+
+
 def solution(mesh):
     return jax.shard_map(
         shards,

time: 770 us -> 689 us (0.89)
  waiting for transfers between devices: 511 us -> 411 us
  matrix products: 75.9 us -> 30.6 us
  Pallas kernels: 0 us -> 28.4 us
  blocking collectives: 126 us -> 144 us
  local copies, waits for them, and re-layouts: 20.4 us -> 36.9 us
    reduce_scatter x6 -> x3, waiting for transfers between devices: 280 us -> 189 us  [sum_rows(): lax.psum_scatter(term, ('wsh', 'ctx'), scatter_dimension=0, tiled=True)]
    psum x1, blocking collectives: 104 us -> 38.7 us  [by_heads(): lax.psum(jnp.stack([grad_gain_one, grad_gain_two]), ('ctx', 'wsh'))]
    all_gather x6 -> x4, waiting for transfers between devices: 228 us -> 170 us  [gather_rows(): return lax.all_gather(mine, ('wsh', 'ctx'), axis=0, tiled=True)]
    unnamed x12 -> x9, waiting for transfers between devices: 2.39 us -> 52.7 us
    all_to_all x0 -> x3, blocking collectives: none -> 49 us  [swap(): return lax.all_to_all(sent, 'ctx', split_axis=0, concat_axis=0, tiled=True)]
    all_gather x1 -> x5, blocking collectives: 9.16 us -> 56.5 us  [the longest x4 50.3 us: sum_rows(): sums = lax.all_gather(piece, 'ctx', axis=0, tiled=True)]
    dot_general x18 -> x12, matrix products: 75.9 us -> 30.6 us  [mm(): lax.dot_general(left, right, dims, preferred_element_type=jnp.float32)]
    pallas_call x0 -> x2, Pallas kernels: none -> 28.4 us  [the longest x1 15.5 us: attend_back(): pl.pallas_call(attend_back_kernel, grid=(pairs, length // rows), in_specs...]
  transfers between devices with their start and end apart: 12 -> 9, of which waited for: 12 -> 7; matrix products, arithmetic and copies ran while one was open for 10% -> 9% of each run, Pallas kernels for 0% -> 4%
where the time goes in v1:
time: 689 us; the launch traced here: 685 us
  waiting for transfers between devices  411 us (60%)
  blocking collectives  144 us (21%)
  local copies, waits for them, and re-layouts  36.9 us (5%)
  matrix products  30.6 us (4%)
  Pallas kernels  28.4 us (4%)
  between operations  14.8 us (2%)
  other arithmetic  14.4 us (2%)
    reduce_scatter x3, waiting for transfers between devices, sum_rows(): lax.psum_scatter(term, ('wsh', 'ctx'), scatter_dimension=0, tiled=True)  189 us
    all_gather x4, waiting for transfers between devices, gather_rows(): return lax.all_gather(mine, ('wsh', 'ctx'), axis=0, tiled=True)  170 us
    unnamed x9, waiting for transfers between devices  52.7 us
    all_gather x4, blocking collectives, sum_rows(): sums = lax.all_gather(piece, 'ctx', axis=0, tiled=True)  50.3 us
    all_to_all x3, blocking collectives, swap(): return lax.all_to_all(sent, 'ctx', split_axis=0, concat_axis=0, tiled=True)  49 us
    psum x1, blocking collectives, by_heads(): lax.psum(jnp.stack([grad_gain_one, grad_gain_two]), ('ctx', 'wsh'))  38.7 us
    dot_general x12, matrix products, mm(): lax.dot_general(left, right, dims, preferred_element_type=jnp.float32)  30.6 us
    unnamed x80, local copies, waits for them, and re-layouts  17.7 us
  transfers between devices with their start and end apart: 9, of which 7 were waited for; matrix products, arithmetic and copies ran while one was open for 9% of the time, Pallas kernels for 4%

profile of v1, /device:TPU:17, one launch (start us, length us, event | category | flops | bytes accessed | tf_op | source)
XLA Modules:
  0.0 685.2 jit_solution(12403534198461214459)
XLA Ops:
  7.2 1.1 copy-done
  9.1 1.5 dynamic-slice_bitcast_fusion
  10.7 1.4 constant_dynamic-slice_fusion.2
  12.1 1.6 constant_dynamic-slice_fusion.1
  13.7 0.7 convert_element_type.128
  14.4 0.7 stack.53
  15.7 6.2 all-gather
  22.6 0.8 multiply_cosine_fusion
  23.6 48.2 %all-gather.7.cloned.1.call-done = bf16[768,2304]{1,0:T(8,128)(2,1)} async-done(((bf16[24,2304]{1,0:T(8,128)(2,1)}), bf16[768,2304]{1,0:T(8,128)(2,1)}) %all-gather.7.cloned.1.call-update) | async-done | bytes 3538960 | tf_op jit(solution)/shard_map/all_gather | solution.py:357
  71.8 3.1 fusion.27
  75.0 0.8 stack.59
  77.2 0.8 copy-done.14
  78.0 2.0 maximum_bitcast_fusion
  80.4 19.5 %all_to_all.20 = bf16[8,592,128]{2,1,0:T(8,128)(2,1)S(1)} all-to-all(bf16[8,592,128]{2,1,0:T(8,128)(2,1)S(1)} %pad_maximum_fusion), channel_id=1, replica_groups=mesh['ctx'=8,'wsh'=4] {'ctx'}, dimensions={0} | all-to-all | bytes 2424832 | tf_op jit(solution)/shard_map/all_to_all | solution.py:396
  100.3 0.9 copy-done.8
  101.7 0.7 slice_convert_fusion.3
  102.6 12.9 %shard_map.152 = (f32[3,64,1024]{2,1,0:T(8,128)S(1)}, f32[3,1024,1024]{2,1,0:T(8,128)}) custom-call(bf16[3,64,1024]{2,1,0:T(8,128)(2,1)S(1)} %reshape.274.q_ref, bf16[3,64,1024]{2,1,0:T(8,128)(2,1)S(1)} %reshape.275.k_ref, bf16[3,64,1024]{2,1,0:T(8,128)(2,1)S(1)} %reshape.276.v_ref, f32[1024,1]{1,0:T(8,128)S(1)} %copy.48.mask_ref), custom_call_target="tpu_custom_call" | custom-call | flops 805306368 | bytes 12582912 | tf_op jit(solution)/shard_map/pallas_call | solution.py:288
  115.7 0.8 copy.79
  116.5 4.2 all-to-all-start.1
  120.7 9.2 %all-gather.13.cloned.1.call-done = bf16[32,36,768]{2,1,0:T(8,128)(2,1)} async-done(((bf16[1,36,768]{2,1,0:T(8,128)(2,1)}), bf16[32,36,768]{2,1,0:T(8,128)(2,1)}) %all-gather.13.cloned.1.call-update) | async-done | bytes 1769488 | tf_op jit(solution)/shard_map/all_gather | solution.py:357
  130.0 3.6 reshape.296
  134.0 52.5 %all-gather.9.cloned.1.call-done = bf16[768,768]{1,0:T(8,128)(2,1)} async-done(((bf16[24,768]{1,0:T(8,128)(2,1)}), bf16[768,768]{1,0:T(8,128)(2,1)}) %all-gather.9.cloned.1.call-update) | async-done | bytes 1179664 | tf_op jit(solution)/shard_map/all_gather | solution.py:357
  186.5 1.9 fusion.26
  189.2 59.8 %all-gather.11.cloned.1.call-done = bf16[768,2304]{1,0:T(8,128)(2,1)} async-done(((bf16[24,2304]{1,0:T(8,128)(2,1)}), bf16[768,2304]{1,0:T(8,128)(2,1)}) %all-gather.11.cloned.1.call-update) | async-done | bytes 3538960 | tf_op jit(solution)/shard_map/all_gather | solution.py:357
  249.0 3.3 fusion.19
  252.3 1.9 fusion.6
  254.3 1.8 multiply_reduce_fusion
  256.6 0.8 copy-done.5
  257.6 0.7 copy-done.15
  258.3 1.5 convolution_convert_fusion.3
  259.9 0.9 copy-done.11
  260.8 3.0 convolution_convert_fusion.2
  263.8 3.8 reshape.287
  267.6 4.7 convolution_convert_fusion
  272.4 0.9 copy-done.16
  273.4 2.5 convolution_convert_fusion.4
  275.9 1.1 reshape_broadcast_in_dim.3
  277.0 10.3 %all_to_all.21 = bf16[8,192,128]{2,1,0:T(8,128)(2,1)S(1)} all-to-all(bf16[8,192,128]{2,1,0:T(8,128)(2,1)S(1)} %bitcast.135), channel_id=1, replica_groups=mesh['ctx'=8,'wsh'=4] {'ctx'}, dimensions={0} | all-to-all | bytes 786432 | tf_op jit(solution)/shard_map/all_to_all | solution.py:396
  287.3 1.0 copy.53
  288.3 1.2 reshape.281.do_ref
  289.5 15.5 %shard_map.153 = (f32[3,64,1024]{2,1,0:T(8,128)S(1)}, f32[3,64,1024]{2,1,0:T(8,128)S(1)}, f32[3,64,1024]{2,1,0:T(8,128)S(1)}) custom-call(bf16[3,64,1024]{2,1,0:T(8,128)(2,1)S(1)} %reshape.274.q_ref, bf16[3,64,1024]{2,1,0:T(8,128)(2,1)S(1)} %reshape.275.k_ref, bf16[3,64,1024]{2,1,0:T(8,128)(2,1)S(1)} %reshape.276.v_ref, ...), custom_call_target="tpu_custom_call" | custom-call | flops 1610612736 | bytes 12582912 | tf_op jit(solution)/shard_map/pallas_call | solution.py:331
  305.8 19.3 %all_to_all.22 = bf16[8,576,128]{2,1,0:T(8,128)(2,1)S(1)} all-to-all(bf16[8,576,128]{2,1,0:T(8,128)(2,1)S(1)} %copy.54), channel_id=1, replica_groups=mesh['ctx'=8,'wsh'=4] {'ctx'}, dimensions={0} | all-to-all | bytes 2359296 | tf_op jit(solution)/shard_map/all_to_all | solution.py:396
  325.0 1.9 fusion.20
  327.2 0.8 copy.78
  329.4 1.0 subtract_convert_fusion.1
  330.6 0.7 copy-done.22
  331.8 3.0 convolution_convert_fusion.1
  335.5 0.8 copy-done.4
  336.4 1.4 fusion
  337.8 0.7 copy-done.7
  338.5 2.5 multiply_reduce_fusion.2
  341.5 38.7 %psum.7 = f32[2,768]{1,0:T(2,128)S(1)} all-reduce(f32[2,768]{1,0:T(2,128)S(1)} %pad_maximum_fusion.9), channel_id=1, replica_groups=mesh['ctx'=8,'wsh'=4] {'ctx','wsh'}, use_global_device_ids=true, to_apply=%region_10.0 | all-reduce | flops 1536 | bytes 12288 | tf_op jit(solution)/shard_map/psum | solution.py:466
  380.9 1.1 add_convert_fusion.1
  382.0 11.5 %all_gather.33 = bf16[192,768]{1,0:T(8,128)(2,1)S(1)} all-gather(bf16[24,768]{1,0:T(8,128)(2,1)} %reduce-scatter.9.cloned.1.call-done), channel_id=1, replica_groups=mesh['ctx'=8,'wsh'=4] {'ctx'}, dimensions={0}, use_global_device_ids=true | all-gather | bytes 331776 | tf_op jit(solution)/shard_map/all_gather | solution.py:365
  393.5 0.9 convert_element_type.148
  394.4 52.5 %reduce-scatter.13.cloned.1.call-done = bf16[72,384]{1,0:T(8,128)(2,1)} async-done(((bf16[2304,384]{1,0:T(8,128)(2,1)}), bf16[72,384]{1,0:T(8,128)(2,1)}) %reduce-scatter.13.cloned.1.call-update) | async-done | bytes 55312
  446.9 12.4 %all_gather.35 = bf16[576,384]{1,0:T(8,128)(2,1)S(1)} all-gather(bf16[72,384]{1,0:T(8,128)(2,1)} %reduce-scatter.13.cloned.1.call-done), channel_id=1, replica_groups=mesh['ctx'=8,'wsh'=4] {'ctx'}, dimensions={0}, use_global_device_ids=true | all-gather | bytes 497664 | tf_op jit(solution)/shard_map/all_gather | solution.py:365
  459.4 1.0 reshape.292
  460.4 95.1 %reduce-scatter.11.cloned.1.call-done = bf16[24,2304]{1,0:T(8,128)(2,1)} async-done(((bf16[768,2304]{1,0:T(8,128)(2,1)}), bf16[24,2304]{1,0:T(8,128)(2,1)}) %reduce-scatter.11.cloned.1.call-update) | async-done | bytes 110608 | tf_op jit(solution)/shard_map/reduce_scatter | solution.py:364
  555.5 13.1 %all_gather.34 = bf16[192,2304]{1,0:T(8,128)(2,1)S(1)} all-gather(bf16[24,2304]{1,0:T(8,128)(2,1)} %reduce-scatter.11.cloned.1.call-done), channel_id=1, replica_groups=mesh['ctx'=8,'wsh'=4] {'ctx'}, dimensions={0}, use_global_device_ids=true | all-gather | bytes 995328 | tf_op jit(solution)/shard_map/all_gather | solution.py:365
  568.6 1.3 convert_element_type.150
  569.9 93.9 %reduce-scatter.7.cloned.1.call-done = bf16[24,2304]{1,0:T(8,128)(2,1)} async-done(((bf16[768,2304]{1,0:T(8,128)(2,1)}), bf16[24,2304]{1,0:T(8,128)(2,1)}) %reduce-scatter.7.cloned.1.call-update) | async-done | bytes 110608 | tf_op jit(solution)/shard_map/reduce_scatter | solution.py:364
  663.8 13.2 %all_gather.32 = bf16[192,2304]{1,0:T(8,128)(2,1)S(1)} all-gather(bf16[24,2304]{1,0:T(8,128)(2,1)} %reduce-scatter.7.cloned.1.call-done), channel_id=1, replica_groups=mesh['ctx'=8,'wsh'=4] {'ctx'}, dimensions={0}, use_global_device_ids=true | all-gather | bytes 995328 | tf_op jit(solution)/shard_map/all_gather | solution.py:365
  677.1 1.3 convert_element_type.146
  (142 shorter events, 12.3 us)
Async XLA Ops:
  7.2 1.2 copy-start
  7.2 14.9 %copy-start.2 = (bf16[2,128,768]{2,1,0:T(8,128)(2,1)S(1)}, bf16[2,128,768]{2,1,0:T(8,128)(2,1)}, u32[]{:S(2)}) copy-start(bf16[2,128,768]{2,1,0:T(8,128)(2,1)} %param.9) | copy-start | bytes 1179652
  7.2 64.6 %all-gather.7.cloned.1.call-start = ((), (), s32[]{:S(2)}) async-start(), calls=%async_computation.8 | async-start | bytes 3649536 | tf_op jit(solution)/shard_map/all_gather | solution.py:357
  9.0 120.9 %all-gather.13.cloned.1.call-start = ((), (), s32[]{:S(2)}) async-start(), calls=%async_computation.14 | async-start | bytes 2027520 | tf_op jit(solution)/shard_map/all_gather | solution.py:357
  10.6 175.9 %all-gather.9.cloned.1.call-start = ((), (), s32[]{:S(2)}) async-start(), calls=%async_computation.9 | async-start | bytes 1216512 | tf_op jit(solution)/shard_map/all_gather | solution.py:357
  12.1 236.9 %all-gather.11.cloned.1.call-start = ((), (), s32[]{:S(2)}) async-start(), calls=%async_computation.10 | async-start | bytes 3649536 | tf_op jit(solution)/shard_map/all_gather | solution.py:357
  22.3 52.7 %copy-start.26 = (f32[256]{0:T(256)}, f32[256]{0:T(256)S(1)}, u32[]{:S(2)}) copy-start(f32[256]{0:T(256)S(1)} %get-tuple-element.54) | copy-start | bytes 3076
  22.5 52.5 %copy-start.32 = (f32[2,128]{1,0:T(2,128)}, f32[2,128]{1,0:T(2,128)S(1)}, u32[]{:S(2)}) copy-start(f32[2,128]{1,0:T(2,128)S(1)} %multiply_reduce_fusion.5) | copy-start | bytes 3076
  22.5 52.4 %copy-start.28 = (f32[256]{0:T(256)}, f32[256]{0:T(256)S(1)}, u32[]{:S(2)}) copy-start(f32[256]{0:T(256)S(1)} %bitcast_rsqrt_fusion) | copy-start | bytes 3076
  23.6 48.2 %copy-start.17 = (bf16[256,768]{1,0:T(8,128)(2,1)}, bf16[256,768]{1,0:T(8,128)(2,1)S(1)}, u32[]{:S(2)}) copy-start(bf16[256,768]{1,0:T(8,128)(2,1)S(1)} %multiply_convert_fusion.2) | copy-start | bytes 1179652
  75.9 0.8 copy-start.24
  75.9 0.8 copy-start.25
  77.0 1.0 copy-start.14
  100.2 1.0 copy-start.8
  116.5 17.1 %all-to-all-start.1 = ((bf16[8,192,128]{2,1,0:T(8,128)(2,1)}), bf16[8,192,128]{2,1,0:T(8,128)(2,1)S(1)}, u32[]{:S(2)}, u32[]{:S(2)}) async-start(bf16[8,192,128]{2,1,0:T(8,128)(2,1)} %bitcast.115), calls=%async_computation.1 | async-start | bytes 786432 | tf_op jit(solution)/shard_map/all_to_all | solution.py:396
  120.7 261.3 %reduce-scatter.9.cloned.1.call-start = ((), (), s32[]{:S(2)}) async-start(), calls=%async_computation.12 | async-start | bytes 1216512 | tf_op jit(solution)/shard_map/reduce_scatter | solution.py:364
  188.6 0.6 copy-start.34
  249.0 3.3 copy-start.3
  249.0 3.3 copy-start.10
  252.3 2.0 copy-start.9
  254.2 1.9 copy-start.19
  254.2 1.9 copy-start.20
  254.3 1.8 copy-start.35
  256.5 0.9 copy-start.5
  256.5 0.9 copy-start.30
  257.6 0.7 copy-start.15
  259.8 1.0 copy-start.11
  259.8 187.1 %reduce-scatter.13.cloned.1.call-start = ((), (), s32[]{:S(2)}) async-start(), calls=%async_computation.15 | async-start | bytes 1824768
  267.6 287.9 %reduce-scatter.11.cloned.1.call-start = ((), (), s32[]{:S(2)}) async-start(), calls=%async_computation.13 | async-start | bytes 3649536 | tf_op jit(solution)/shard_map/reduce_scatter | solution.py:364
  272.4 1.0 copy-start.16
  272.4 391.4 %reduce-scatter.7.cloned.1.call-start = ((), (), s32[]{:S(2)}) async-start(), calls=%async_computation.11 | async-start | bytes 3649536 | tf_op jit(solution)/shard_map/reduce_scatter | solution.py:364
  330.4 1.1 copy-start.18
  330.4 1.4 copy-start.21
  330.5 0.7 copy-start.22
  330.5 4.2 copy-start.23
  334.8 0.7 copy-start.36
  334.8 1.5 copy-start.4
  334.8 1.6 copy-start.13
  334.8 3.0 copy-start.27
  336.4 2.1 copy-start.7
  338.5 2.5 copy-start.33
  338.5 2.5 copy-start.29
  341.0 39.9 %copy-start.6 = (f32[256,768]{1,0:T(8,128)S(1)}, f32[256,768]{1,0:T(8,128)}, u32[]{:S(2)}) copy-start(f32[256,768]{1,0:T(8,128)} %copy-done.5) | copy-start | bytes 2359300
  341.0 39.9 %copy-start.12 = (bf16[2,128,768]{2,1,0:T(8,128)(2,1)S(1)}, bf16[2,128,768]{2,1,0:T(8,128)(2,1)}, u32[]{:S(2)}) copy-start(bf16[2,128,768]{2,1,0:T(8,128)(2,1)} %param.17) | copy-start | bytes 1179652
  341.0 39.8 %copy-start.31 = (f32[256]{0:T(256)S(1)}, f32[256]{0:T(256)}, u32[]{:S(2)}) copy-start(f32[256]{0:T(256)} %copy-done.30) | copy-start | bytes 3076
  663.8 14.6 %copy-start.1 = (bf16[192,2304]{1,0:T(8,128)(2,1)S(1)}, bf16[192,2304]{1,0:T(8,128)(2,1)}, u32[]{:S(2)}) copy-start(bf16[192,2304]{1,0:T(8,128)(2,1)} %param.11) | copy-start | bytes 2654212
Sparse Core Ops, SparseCore 0:
  11.5 60.2 all-gather.6
  75.3 54.6 all-gather.12
  133.4 53.0 all-gather.8
  189.9 59.0 all-gather.10
  260.0 93.2 reduce-scatter.8
  358.4 88.4 reduce-scatter.12
  453.2 102.1 reduce-scatter.10
  561.8 101.9 reduce-scatter.6

commit v2 on v1

--- a/solution.py
+++ b/solution.py
@@ -1,3 +1,4 @@
+import functools
 import math
 
 import jax
@@ -350,20 +351,447 @@
     )(queries, keys, values, grad_out, mixed, prob)
 
 
-def gather_rows(part):
-    pieces = lax.axis_size("ctx")
-    rows = part.shape[0] // pieces
-    mine = lax.dynamic_slice_in_dim(part, lax.axis_index("ctx") * rows, rows, 0)
-    return lax.all_gather(mine, ("wsh", "ctx"), axis=0, tiled=True)
-
-
-def sum_rows(term):
-    total, width = term.shape
-    fold = 2 if total % 256 else 1
-    term = term.astype(jnp.bfloat16).reshape(total * fold, width // fold)
-    piece = lax.psum_scatter(term, ("wsh", "ctx"), scatter_dimension=0, tiled=True)
-    sums = lax.all_gather(piece, "ctx", axis=0, tiled=True)
-    return sums.reshape(-1, width).astype(jnp.float32)
+MESH = pl.DeviceIdType.MESH
+CTX = 8
+TILE = 16
+
+
+class Place:
+    def __init__(self):
+        self.c, self.z = lax.axis_index("ctx"), lax.axis_index("wsh")
+        self.core = lax.rem(self.c, 2)
+        self.x = lax.rem(self.c // 2, 2)
+        self.y = self.c // 4
+
+    def flip(self, core=0, x=0, y=0):
+        core = 1 - self.core if core else self.core
+        x = 1 - self.x if x else self.x
+        y = 1 - self.y if y else self.y
+        return core, x, y
+
+    def device(self, **axes):
+        core, x, y = self.flip(**axes)
+        return (y * 4 + x * 2 + core, self.z)
+
+    def chip(self, **axes):
+        core, x, y = self.flip(**axes)
+        return y * 2 + x
+
+    def piece(self, **axes):
+        core, x, y = self.flip(**axes)
+        return core * 4 + y * 2 + x
+
+
+def greet(me, depth):
+    barrier = pltpu.get_barrier_semaphore()
+    for axes in ({"core": 1}, {"x": 1}, {"y": 1}):
+        pl.semaphore_signal(barrier, inc=1, device_id=me.device(**axes), device_id_type=MESH)
+
+    @pl.when(me.z > 0)
+    def _():
+        pl.semaphore_signal(barrier, inc=1, device_id=(me.c, me.z - 1), device_id_type=MESH)
+
+    @pl.when(me.z < depth - 1)
+    def _():
+        pl.semaphore_signal(barrier, inc=1, device_id=(me.c, me.z + 1), device_id_type=MESH)
+
+    line_peers = jnp.where(me.z > 0, 1, 0) + jnp.where(me.z < depth - 1, 1, 0)
+    pl.semaphore_wait(barrier, 3 + line_peers)
+
+
+def remote(src, dst, send, recv, device):
+    return pltpu.make_async_remote_copy(
+        src_ref=src, dst_ref=dst, send_sem=send, recv_sem=recv, device_id=device, device_id_type=MESH
+    )
+
+
+def rows_at(start, count):
+    return pl.ds(pl.multiple_of(start, TILE), count)
+
+
+def cut(size):
+    first = (size // TILE + 1) // 2 * TILE
+    return first, size - first
+
+
+SPREAD = 9
+X, Y, XY = {"x": 1}, {"y": 1}, {"x": 1, "y": 1}
+CORE = {"core": 1}
+
+
+def spread(me, size, own, buf, send, recv):
+    first, second = cut(size)
+    whole, one, two = (0, size), (0, first), (first, second)
+    moves = (
+        ({}, whole, X),
+        ({}, whole, Y),
+        ({}, whole, CORE),
+        (X, one, Y),
+        (X, whole, CORE),
+        (Y, two, X),
+        (Y, whole, CORE),
+        (XY, one, CORE),
+        (XY, two, CORE),
+    )
+
+    def region(axes, part):
+        return buf(me.piece(**axes) * size + part[0], part[1])
+
+    def sent(i):
+        axes, part, to = moves[i]
+        here = own if not axes else region(axes, part)
+        return remote(here, region(axes, part), send(i), recv(i), me.device(**to))
+
+    def arrived(i):
+        axes, part, to = moves[i]
+        source = {key: 1 for key in ("core", "x", "y") if (key in axes) != (key in to)}
+        there = region(source, part)
+        remote(there, there, send(i), recv(i), me.device(**to)).wait_recv()
+
+    def begin():
+        for i in (0, 1, 2):
+            sent(i).start()
+
+    def middle():
+        arrived(0)
+        sent(3).start()
+        sent(4).start()
+        arrived(1)
+        sent(5).start()
+        sent(6).start()
+
+    def late():
+        arrived(3)
+        sent(7).start()
+        arrived(5)
+        sent(8).start()
+
+    def finish():
+        for i in (2, 4, 6, 7, 8):
+            arrived(i)
+        for i in range(SPREAD):
+            sent(i).wait_send()
+
+    return begin, middle, late, finish
+
+
+def layout(arrays, lead, width):
+    plan, start = [], 0
+    for n, array in enumerate(arrays):
+        rows = array.shape[0] // lead
+        for i in range(array.shape[1] // width):
+            plan.append((n, i * width, rows, start))
+            start += rows
+    return plan, start
+
+
+def gather_kernel(count, *refs):
+    parts, out = refs[:count], refs[count]
+    line_send, line_recv, send, recv, local = refs[count + 1 :]
+    depth, total, width = out.shape
+    size = total // CTX
+    me = Place()
+    plan, used = layout(parts, 1, width)
+    keeps = [
+        pltpu.make_async_copy(
+            parts[n].at[:, pl.ds(column, width)], out.at[me.z, pl.ds(start, rows)], local.at[m]
+        )
+        for m, (n, column, rows, start) in enumerate(plan)
+    ]
+    for keep in keeps:
+        keep.start()
+    greet(me, depth)
+    for keep in keeps:
+        keep.wait()
+    mine = rows_at(me.piece() * size, size)
+
+    def along(way, t):
+        origin, to = (me.z - t, me.z + 1) if way == 0 else (me.z + t, me.z - 1)
+        origin, to = jnp.clip(origin, 0, depth - 1), jnp.clip(to, 0, depth - 1)
+        here = out.at[origin, mine]
+        pair = (line_send.at[way, t], line_recv.at[way, t])
+        return remote(here, out.at[origin, mine], *pair, (me.c, to))
+
+    def goes(way, t):
+        if way == 0:
+            return (me.z >= t) & (me.z + 1 < depth)
+        return (me.z + t < depth) & (me.z >= 1)
+
+    def comes(way, t):
+        return me.z >= t if way == 0 else me.z + t < depth
+
+    def steps(way, t):
+        origin = jnp.clip(me.z - t if way == 0 else me.z + t, 0, depth - 1)
+        slot = way * (depth - 1) + t - 1
+        return spread(
+            me,
+            size,
+            out.at[origin, mine],
+            lambda start, count: out.at[origin, rows_at(start, count)],
+            lambda i: send.at[slot, i],
+            lambda i: recv.at[slot, i],
+        )
+
+    for way in (0, 1):
+
+        @pl.when(goes(way, 0))
+        def _():
+            along(way, 0).start()
+
+    for t in range(1, depth + 2):
+        for way in (0, 1):
+            if t < depth:
+
+                @pl.when(comes(way, t))
+                def _():
+                    origin = jnp.clip(me.z - t if way == 0 else me.z + t, 0, depth - 1)
+                    there = out.at[origin, mine]
+                    pair = (line_send.at[way, t - 1], line_recv.at[way, t - 1])
+                    remote(there, there, *pair, me.device(**X)).wait_recv()
+                    if t < depth - 1:
+
+                        @pl.when(goes(way, t))
+                        def _():
+                            along(way, t).start()
+
+                    steps(way, t)[0]()
+
+        for way in (0, 1):
+            if 1 <= t - 1 < depth:
+
+                @pl.when(comes(way, t - 1))
+                def _():
+                    steps(way, t - 1)[1]()
+
+        for way in (0, 1):
+            if 1 <= t - 2 < depth:
+
+                @pl.when(comes(way, t - 2))
+                def _():
+                    steps(way, t - 2)[2]()
+
+    for way in (0, 1):
+        for t in range(1, depth):
+
+            @pl.when(comes(way, t))
+            def _():
+                steps(way, t)[3]()
+
+        for t in range(depth - 1):
+
+            @pl.when(goes(way, t))
+            def _():
+                along(way, t).wait_send()
+
+
+def gather_packed(parts, width):
+    depth = lax.axis_size("wsh")
+    dma = pltpu.SemaphoreType.DMA
+    plan, used = layout(parts, 1, width)
+    return pl.pallas_call(
+        functools.partial(gather_kernel, len(parts)),
+        out_shape=jax.ShapeDtypeStruct((depth, used, width), parts[0].dtype),
+        in_specs=[pl.BlockSpec(memory_space=pl.ANY)] * len(parts),
+        out_specs=pl.BlockSpec(memory_space=pl.ANY),
+        scratch_shapes=[
+            dma((2, depth - 1)),
+            dma((2, depth - 1)),
+            dma((2 * (depth - 1), SPREAD)),
+            dma((2 * (depth - 1), SPREAD)),
+            dma((len(plan),)),
+        ],
+        compiler_params=pltpu.CompilerParams(collective_id=1, has_side_effects=True),
+    )(*parts)
+
+
+def add_rows(total, start, terms, count):
+    def body(i, carry):
+        at = rows_at(start + i * TILE, TILE)
+        value = total[at, :].astype(jnp.float32)
+        for ref, base in terms:
+            value = value + ref[rows_at(base + i * TILE, TILE), :].astype(jnp.float32)
+        total[at, :] = value.astype(total.dtype)
+        return carry
+
+    lax.fori_loop(0, count // TILE, body, 0)
+
+
+def reduce_kernel(count, *refs):
+    parts, out = refs[:count], refs[count]
+    total, pair, near_x, near_y, last, line = refs[count + 1 : count + 7]
+    local, core_send, core_recv, near_send, near_recv = refs[count + 7 : count + 12]
+    line_send, line_recv, send, recv, keep_sem = refs[count + 12 :]
+    depth, size, width = last.shape
+    half = 4 * size
+    first, second = cut(size)
+    me = Place()
+    k, kx, ky, kd = me.chip(), me.chip(**X), me.chip(**Y), me.chip(**XY)
+    to_x, to_y, to_core = me.device(**X), me.device(**Y), me.device(**CORE)
+
+    def cores(zz):
+        return remote(
+            total.at[zz, rows_at((1 - me.core) * half, half)],
+            pair.at[zz],
+            core_send.at[zz],
+            core_recv.at[zz],
+            to_core,
+        )
+
+    plan, used = layout(parts, depth, width)
+    base = me.core * half
+
+    def own(zz):
+        return [
+            pltpu.make_async_copy(
+                parts[n].at[pl.ds(zz * rows, rows), pl.ds(column, width)],
+                total.at[zz, pl.ds(start, rows)],
+                local.at[zz, m],
+            )
+            for m, (n, column, rows, start) in enumerate(plan)
+        ]
+
+    def near(zz, i):
+        sems = (near_send.at[zz, i], near_recv.at[zz, i])
+        part = lambda chip, offset, count: total.at[zz, rows_at(base + chip * size + offset, count)]
+        if i == 0:
+            return remote(part(kd, 0, first), near_x.at[zz, 1], *sems, to_x)
+        if i == 1:
+            return remote(part(kd, first, second), near_y.at[zz, 1], *sems, to_y)
+        if i == 2:
+            return remote(part(kx, 0, first), near_x.at[zz, 0], *sems, to_x)
+        if i == 3:
+            return remote(part(ky, first, second), near_y.at[zz, 0], *sems, to_y)
+        if i == 4:
+            return remote(part(ky, 0, first), last.at[zz, pl.ds(0, first)], *sems, to_y)
+        return remote(part(kx, first, second), last.at[zz, pl.ds(first, second)], *sems, to_x)
+
+    for zz in range(depth):
+        for copy in own(zz):
+            copy.start()
+    greet(me, depth)
+    for zz in range(depth):
+        for copy in own(zz):
+            copy.wait()
+        cores(zz).start()
+    for t in range(depth + 2):
+        if t < depth:
+            cores(t).wait_recv()
+            add_rows(total.at[t], base, [(pair.at[t], 0)], half)
+            for i in range(4):
+                near(t, i).start()
+        if 0 <= t - 1 < depth:
+            zz = t - 1
+            near(zz, 0).wait_recv()
+            add_rows(total.at[zz], base + ky * size, [(near_x.at[zz, 1], 0)], first)
+            near(zz, 4).start()
+            near(zz, 1).wait_recv()
+            add_rows(total.at[zz], base + kx * size + first, [(near_y.at[zz, 1], 0)], second)
+            near(zz, 5).start()
+        if 0 <= t - 2 < depth:
+            zz = t - 2
+            near(zz, 2).wait_recv()
+            near(zz, 4).wait_recv()
+            add_rows(total.at[zz], base + k * size, [(near_x.at[zz, 0], 0), (last.at[zz], 0)], first)
+            near(zz, 3).wait_recv()
+            near(zz, 5).wait_recv()
+            terms = [(near_y.at[zz, 0], 0), (last.at[zz], first)]
+            add_rows(total.at[zz], base + k * size + first, terms, second)
+
+    mine = rows_at(base + k * size, size)
+
+    def along(way, zz):
+        to = jnp.clip(me.z - 1 if way == 0 else me.z + 1, 0, depth - 1)
+        sems = (line_send.at[way, zz], line_recv.at[way, zz])
+        return remote(total.at[zz, mine], line.at[way, zz], *sems, (me.c, to))
+
+    def goes(way, zz):
+        return zz < me.z if way == 0 else zz > me.z
+
+    def fed(way):
+        return me.z + 1 < depth if way == 0 else me.z >= 1
+
+    def take(way, zz):
+        @pl.when(fed(way))
+        def _():
+            along(way, zz).wait_recv()
+            add_rows(total.at[zz], base + k * size, [(line.at[way, zz], 0)], size)
+
+    for j in range(depth):
+        for way, zz in ((0, j), (1, depth - 1 - j)):
+
+            @pl.when(goes(way, zz))
+            def _():
+                take(way, zz)
+                along(way, zz).start()
+
+    take(0, me.z)
+    take(1, me.z)
+    done = total.at[me.z, mine]
+    begin, middle, late, finish = spread(
+        me,
+        size,
+        done,
+        lambda start, count: out.at[rows_at(start, count)],
+        lambda i: send.at[i],
+        lambda i: recv.at[i],
+    )
+    begin()
+    keep = pltpu.make_async_copy(done, out.at[rows_at(me.piece() * size, size)], keep_sem)
+    keep.start()
+    middle()
+    late()
+    finish()
+    keep.wait()
+    for zz in range(depth):
+        cores(zz).wait_send()
+        for i in range(6):
+            near(zz, i).wait_send()
+        for way in (0, 1):
+
+            @pl.when(goes(way, zz))
+            def _():
+                along(way, zz).wait_send()
+
+
+def reduce_packed(parts, width):
+    depth = lax.axis_size("wsh")
+    plan, rows = layout(parts, depth, width)
+    size = rows // CTX
+    first, second = cut(size)
+    dma = pltpu.SemaphoreType.DMA
+    low = parts[0].dtype
+    return pl.pallas_call(
+        functools.partial(reduce_kernel, len(parts)),
+        out_shape=jax.ShapeDtypeStruct((rows, width), low),
+        in_specs=[pl.BlockSpec(memory_space=pl.ANY)] * len(parts),
+        out_specs=pl.BlockSpec(memory_space=pl.ANY),
+        scratch_shapes=[
+            pltpu.VMEM((depth, rows, width), low),
+            pltpu.VMEM((depth, 4 * size, width), low),
+            pltpu.VMEM((depth, 2, first, width), low),
+            pltpu.VMEM((depth, 2, second, width), low),
+            pltpu.VMEM((depth, size, width), low),
+            pltpu.VMEM((2, depth, size, width), low),
+            dma((depth, len(plan))),
+            dma((depth,)),
+            dma((depth,)),
+            dma((depth, 6)),
+            dma((depth, 6)),
+            dma((2, depth)),
+            dma((2, depth)),
+            dma((SPREAD,)),
+            dma((SPREAD,)),
+            dma,
+        ],
+        compiler_params=pltpu.CompilerParams(
+            collective_id=2, has_side_effects=True, vmem_limit_bytes=48 * 2**20
+        ),
+    )(*parts)
+
+
+def spare_rows(used):
+    step = CTX * TILE
+    return (used + 2 + step - 1) // step * step - used
 
 
 def by_heads(tokens, key_mask, w_qkv, w_attn_out, w_in, w_out, attn_gain, mlp_gain, cotangent):
@@ -378,12 +806,37 @@
     tokens_here = seqs * rows
     low = jnp.bfloat16
 
-    gains = lax.all_gather(jnp.stack([attn_gain, mlp_gain]), "wsh", axis=1, tiled=True)
-    gain_one, gain_two = gains[0], gains[1]
-    full_qkv = gather_rows(w_qkv)
-    full_attn = gather_rows(w_attn_out)
-    full_in = gather_rows(w_in)
-    full_out = gather_rows(w_out)
+    depth = lax.axis_size("wsh")
+    share, shape_out = w_qkv.shape[0], w_out.shape
+    blocks = w_qkv.shape[1] // width
+    blocks_in = w_in.shape[1] // width
+
+    used = (blocks + 1 + blocks_in) * share + shape_out[0]
+    spare = spare_rows(used)
+    gain_rows = jnp.pad(
+        jnp.stack([attn_gain, mlp_gain]), ((0, spare - 2), (0, width - share))
+    )
+    packed = gather_packed([w_qkv, w_attn_out, w_in, w_out, gain_rows], width)
+
+    def unfold(start, rows_each, count):
+        return jnp.concatenate(
+            [
+                packed[:, start + i * rows_each : start + (i + 1) * rows_each].reshape(-1, width)
+                for i in range(count)
+            ],
+            axis=1,
+        )
+
+    at_attn = blocks * share
+    at_in = at_attn + share
+    at_out = at_in + blocks_in * share
+    at_gain = at_out + shape_out[0]
+    full_qkv = unfold(0, share, blocks)
+    full_attn = unfold(at_attn, share, 1)
+    full_in = unfold(at_in, share, blocks_in)
+    full_out = unfold(at_out, shape_out[0], 1)
+    gain_one = packed[:, at_gain, :share].reshape(-1)
+    gain_two = packed[:, at_gain + 1, :share].reshape(-1)
 
     def to_heads(parts):
         count = parts.shape[0]
@@ -445,44 +898,53 @@
     gated = gated_f.astype(low)
     outcome = (hidden + mm(gated, full_out)).astype(low).reshape(seqs, rows, width)
     grad_out = cotangent.reshape(tokens_here, width)
-    grad_w_out = sum_rows(mm(gated, grad_out, TN))
+    term_out = mm(gated, grad_out, TN).astype(low)
     (grad_proj,) = glu_pull(mm(grad_out, full_out, NT))
     grad_proj = grad_proj.astype(low)
-    grad_w_in = sum_rows(mm(normed_two, grad_proj, TN))
+    term_in = mm(normed_two, grad_proj, TN).astype(low)
     grad_hidden_ln, grad_gain_two = norm_two_pull(mm(grad_proj, full_in, NT))
     grad_hidden = grad_out.astype(jnp.float32) + grad_hidden_ln
     grad_branch = grad_hidden.astype(low)
-    grad_w_attn = sum_rows(mm(attended, grad_branch, TN))
+    term_attn = mm(attended, grad_branch, TN).astype(low)
     grad_att = mm(full_attn, grad_branch, NT).astype(low)
     got_do = swap(to_heads(grad_att[None]))
     got_do = jnp.transpose(got_do, (1, 0, 2)).reshape(pairs, head_width, length)
     grads = attend_back(queries, keys, values, got_do, mixed, prob)
     back = to_rows(jnp.stack([g.reshape(feats, length) for g in grads])).astype(jnp.float32)
     grad_joined = jnp.concatenate([turn(back[0], -1.0), turn(back[1], -1.0), back[2]]).astype(low)
-    grad_w_qkv = sum_rows(mm(normed, grad_joined, (((0,), (1,)), ((), ()))))
+    term_qkv = mm(normed, grad_joined, (((0,), (1,)), ((), ()))).astype(low)
     grad_normed = mm(grad_joined, full_qkv, (((0,), (1,)), ((), ())))
     grad_in_ln, grad_gain_one = norm_one_pull(grad_normed)
     grad_tokens = (grad_hidden + grad_in_ln).astype(low).reshape(seqs, rows, width)
-    gain_sums = lax.psum(jnp.stack([grad_gain_one, grad_gain_two]), ("ctx", "wsh"))
-    share = attn_gain.shape[0]
-    gain_sums = lax.dynamic_slice_in_dim(gain_sums, lax.axis_index("wsh") * share, share, 1)
+    gain_terms = jnp.stack([grad_gain_one, grad_gain_two]).astype(low)
+    gain_terms = jnp.transpose(gain_terms.reshape(2, depth, share), (1, 0, 2))
+
+    gain_terms = jnp.pad(gain_terms, ((0, 0), (0, spare - 2), (0, width - share)))
+    terms = [term_qkv, term_attn, term_in, term_out, gain_terms.reshape(-1, width)]
+    sums = reduce_packed(terms, width).astype(jnp.float32)
+
+    def side(start, count):
+        return jnp.concatenate(
+            [sums[start + i * share : start + (i + 1) * share] for i in range(count)], axis=1
+        )
+
     return (
         outcome,
         grad_tokens,
-        gain_sums[0],
-        gain_sums[1],
-        grad_w_qkv,
-        grad_w_attn,
-        grad_w_in,
-        grad_w_out,
+        sums[at_gain, :share],
+        sums[at_gain + 1, :share],
+        side(0, blocks),
+        side(at_attn, 1),
+        side(at_in, blocks_in),
+        sums[at_out : at_out + shape_out[0]],
     )
 
 
 def shards(*arrays):
     seqs = arrays[0].shape[0]
     peers = lax.axis_size("ctx")
-    even = (seqs * HEADS) % peers == 0 and peers % seqs == 0
-    even = even and all(w.shape[0] % peers == 0 for w in arrays[2:6])
+    even = (seqs * HEADS) % peers == 0 and peers % seqs == 0 and peers == CTX
+    even = even and lax.axis_size("wsh") > 1 and arrays[4].shape[1] % arrays[0].shape[2] == 0
     return (by_heads if even else by_positions)(*arrays)
 
 

time: 689 us -> 380 us (0.55)
  waiting for transfers between devices: 411 us -> 8.03 us
  Pallas kernels: 28.4 us -> 255 us
  blocking collectives: 144 us -> 31.1 us
  between operations: 14.8 us -> 1.27 us
  matrix products: 30.6 us -> 22.3 us
    pallas_call x0 -> x2, Pallas kernels: none -> 226 us  [the longest x1 124 us: gather_packed(): pl.pallas_call(functools.partial(gather_kernel, len(parts)), out_shape=ja...]
    reduce_scatter x3 -> x0, waiting for transfers between devices: 189 us -> none  [sum_rows(): lax.psum_scatter(term, ('wsh', 'ctx'), scatter_dimension=0, tiled=True)]
    all_gather x4 -> x0, waiting for transfers between devices: 170 us -> none  [gather_rows(): return lax.all_gather(mine, ('wsh', 'ctx'), axis=0, tiled=True)]
    all_gather x5 -> x0, blocking collectives: 56.5 us -> none  [the longest x4 50.3 us: sum_rows(): sums = lax.all_gather(piece, 'ctx', axis=0, tiled=True)]
    unnamed x9 -> x0, waiting for transfers between devices: 52.7 us -> none
    psum x1 -> x0, blocking collectives: 38.7 us -> none  [by_heads(): lax.psum(jnp.stack([grad_gain_one, grad_gain_two]), ('ctx', 'wsh'))]
    all_to_all x3 -> x2, blocking collectives: 49 us -> 31.1 us  [swap(): return lax.all_to_all(sent, 'ctx', split_axis=0, concat_axis=0, tiled=True)]
    unnamed x80 -> x68, local copies, waits for them, and re-layouts: 17.7 us -> 6.21 us
  transfers between devices with their start and end apart: 9 -> 2, of which waited for: 7 -> 2; matrix products, arithmetic and copies ran while one was open for 9% -> 3% of each run, Pallas kernels for 4% -> 0%
where the time goes in v2:
time: 380 us; the launch traced here: 379 us
  Pallas kernels  255 us (67%)
  local copies, waits for them, and re-layouts  36.2 us (10%)
  blocking collectives  31.1 us (8%)
  matrix products  22.3 us (6%)
  other arithmetic  16 us (4%)
  starting transfers between devices  9.38 us (2%)
  waiting for transfers between devices  8.03 us (2%)
    pallas_call x1, Pallas kernels, gather_packed(): pl.pallas_call(functools.partial(gather_kernel, len(parts)), out_shape=ja...  124 us
    pallas_call x1, Pallas kernels, reduce_packed(): pl.pallas_call(functools.partial(reduce_kernel, len(parts)), out_shape=ja...  103 us
    all_to_all x2, blocking collectives, swap(): return lax.all_to_all(sent, 'ctx', split_axis=0, concat_axis=0, tiled=True)  31.1 us
    dot_general x12, matrix products, mm(): lax.dot_general(left, right, dims, preferred_element_type=jnp.float32)  22.3 us
    pallas_call x1, Pallas kernels, attend_back(): pl.pallas_call(attend_back_kernel, grid=(pairs, length // rows), in_specs...  15.4 us
    pallas_call x1, Pallas kernels, attend(): pl.pallas_call(attend_kernel, grid=(pairs, length // rows), in_specs=[par...  12.9 us
    all_to_all x2, starting transfers between devices, swap(): return lax.all_to_all(sent, 'ctx', split_axis=0, concat_axis=0, tiled=True)  9.38 us
    slice x2, local copies, waits for them, and re-layouts, unfold(): packed[:, start + i * rows_each:start + (i + 1) * rows_each]  8.48 us
  transfers between devices with their start and end apart: 2, of which 2 were waited for; matrix products, arithmetic and copies ran while one was open for 3% of the time, Pallas kernels for 0%

profile of v2, /device:TPU:17, one launch (start us, length us, event | category | flops | bytes accessed | tf_op | source)
XLA Modules:
  0.0 379.2 jit_solution(23662845775565737)
XLA Ops:
  0.6 0.7 stack.56
  1.3 0.7 stack.57
  2.0 0.6 fusion.17.refs_4_
  2.6 123.8 %shard_map.152 = bf16[4,1664,768]{2,1,0:T(8,128)(2,1)} custom-call(bf16[192,2304]{1,0:T(8,128)(2,1)} %refs_0_.1, bf16[192,768]{1,0:T(8,128)(2,1)} %refs_1_.1, bf16[192,2304]{1,0:T(8,128)(2,1)} %refs_2_.1, bf16[288,768]{1,0:T(8,128)(2,1)} %refs_3_.1, bf16[32,768]{1,0:T(8,128)(2,1)} %fusion.17.refs_4_), custom_call_target="tpu_custom_call" | custom-call | tf_op jit(solution)/shard_map/pallas_call | solution.py:591
  126.4 0.8 convert_reduce_fusion.1
  127.3 5.7 %fusion.30 = (bf16[4,192,768]{2,1,0:T(8,128)(2,1)}, bf16[4,192,768]{2,1,0:T(8,128)(2,1)}, bf16[4,192,768]{2,1,0:T(8,128)(2,1)}, bf16[4,192,768]{2,1,0:T(8,128)(2...) fusion(bf16[4,1664,768]{2,1,0:T(8,128)(2,1)} %shard_map.152), kind=kLoop, calls=%fused_computation.104 | loop fusion | bytes 16515072 | tf_op jit(solution)/shard_map/slice | solution.py:824
  133.1 0.2 multiply_reduce_fusion.5
  133.7 0.4 copy-done.18
  134.0 2.4 fusion.3
  136.7 0.5 copy-done.31
  137.5 0.2 subtract_convert_fusion.3
  138.0 2.0 maximum_bitcast_fusion
  140.1 0.2 copy.46
  140.4 19.0 %all_to_all.20 = bf16[8,592,128]{2,1,0:T(8,128)(2,1)S(1)} all-to-all(bf16[8,592,128]{2,1,0:T(8,128)(2,1)S(1)} %pad_maximum_fusion.8), channel_id=1, replica_groups=mesh['ctx'=8,'wsh'=4] {'ctx'}, dimensions={0} | all-to-all | bytes 2424832 | tf_op jit(solution)/shard_map/all_to_all | solution.py:849
  159.4 0.3 copy.79
  160.6 12.9 %shard_map.153 = (f32[3,64,1024]{2,1,0:T(8,128)S(1)}, f32[3,1024,1024]{2,1,0:T(8,128)}) custom-call(bf16[3,64,1024]{2,1,0:T(8,128)(2,1)S(1)} %reshape.315.q_ref, bf16[3,64,1024]{2,1,0:T(8,128)(2,1)S(1)} %reshape.316.k_ref, bf16[3,64,1024]{2,1,0:T(8,128)(2,1)S(1)} %reshape.317.v_ref, f32[1024,1]{1,0:T(8,128)S(1)} %copy.48.mask_ref), custom_call_target="tpu_custom_call" | custom-call | flops 805306368 | bytes 12582912 | tf_op jit(solution)/shard_map/pallas_call | solution.py:289
  173.6 0.8 copy.81
  174.4 4.2 %all-to-all-start.1 = ((bf16[8,192,128]{2,1,0:T(8,128)(2,1)}), bf16[8,192,128]{2,1,0:T(8,128)(2,1)S(1)}, u32[]{:S(2)}, u32[]{:S(2)}) async-start(bf16[8,192,128]{2,1,0:T(8,128)(2,1)} %bitcast.112), calls=%async_computation.1 | async-start | bytes 786432 | tf_op jit(solution)/shard_map/all_to_all | solution.py:849
  178.7 2.8 slice.151
  181.5 3.2 all-to-all-done.1
  184.7 0.4 copy.50
  185.2 2.0 fusion.36
  187.2 0.2 multiply_reduce_fusion.4
  187.6 1.1 fusion.1
  188.8 0.3 copy-done.3
  189.2 1.9 fusion.9
  191.1 1.2 multiply_reduce_fusion
  192.5 0.3 fusion.29
  193.1 0.8 copy-done.14
  193.9 0.7 copy-done.7
  194.6 1.2 convolution_convert_fusion.4
  195.8 1.8 reshape_broadcast_in_dim.3
  197.7 1.0 copy.52
  198.7 12.2 %all_to_all.21 = bf16[8,192,128]{2,1,0:T(8,128)(2,1)S(1)} all-to-all(bf16[8,192,128]{2,1,0:T(8,128)(2,1)S(1)} %bitcast.136), channel_id=1, replica_groups=mesh['ctx'=8,'wsh'=4] {'ctx'}, dimensions={0} | all-to-all | bytes 786432 | tf_op jit(solution)/shard_map/all_to_all | solution.py:849
  210.9 1.0 copy.53
  211.9 1.2 reshape.327.do_ref
  213.1 15.4 %shard_map.154 = (f32[3,64,1024]{2,1,0:T(8,128)S(1)}, f32[3,64,1024]{2,1,0:T(8,128)S(1)}, f32[3,64,1024]{2,1,0:T(8,128)S(1)}) custom-call(bf16[3,64,1024]{2,1,0:T(8,128)(2,1)S(1)} %reshape.315.q_ref, bf16[3,64,1024]{2,1,0:T(8,128)(2,1)S(1)} %reshape.316.k_ref, bf16[3,64,1024]{2,1,0:T(8,128)(2,1)S(1)} %reshape.317.v_ref, ...), custom_call_target="tpu_custom_call" | custom-call | flops 1610612736 | bytes 12582912 | tf_op jit(solution)/shard_map/pallas_call | solution.py:332
  228.8 0.3 copy.61
  229.2 1.2 copy.54
  230.4 5.2 %all-to-all-start.3 = ((bf16[8,576,128]{2,1,0:T(8,128)(2,1)}), bf16[8,576,128]{2,1,0:T(8,128)(2,1)}, u32[]{:S(2)}, u32[]{:S(2)}) async-start(bf16[8,576,128]{2,1,0:T(8,128)(2,1)} %copy.54), calls=%async_computation.3 | async-start | bytes 2359296 | tf_op jit(solution)/shard_map/all_to_all | solution.py:849
  235.5 0.5 convolution_convert_fusion.3.refs_1_
  236.1 2.0 convolution_convert_fusion.2.refs_3_
  238.2 2.7 fusion.4
  240.8 3.0 convolution_convert_fusion.refs_2_
  243.8 4.9 %all-to-all-done.3 = bf16[8,576,128]{2,1,0:T(8,128)(2,1)} async-done(((bf16[8,576,128]{2,1,0:T(8,128)(2,1)}), bf16[8,576,128]{2,1,0:T(8,128)(2,1)}, u32[]{:S(2)}, u32[]{:S(2)}) %all-to-all-start.3) | async-done | bytes 1179680 | tf_op jit(solution)/shard_map/all_to_all | solution.py:849
  248.7 4.1 %fusion.28 = (f32[3,4,192,2,128]{4,3,2,1,0:T(2,128)S(1)}, bf16[3,4,192,2,128]{4,3,2,1,0:T(2,128)(2,1)}) fusion(bf16[2,4,3,192,128]{4,3,2,1,0:T(8,128)(2,1)} %bitcast.32), kind=kLoop, calls=%fused_computation.102 | loop fusion | flops 589824 | bytes 4718592 | tf_op jit(solution)/shard_map/convert_element_type | solution.py:913
  252.8 1.3 fusion.33
  254.1 2.7 reshape_squeeze.8
  256.7 1.3 slice.188
  258.0 0.8 copy.80
  258.8 2.6 reshape_squeeze.9
  261.5 1.8 subtract_convert_fusion.1
  263.6 1.0 copy-done.17
  264.7 1.2 multiply_reduce_fusion.2
  265.9 2.9 convolution_convert_fusion.1.refs_0_
  268.9 0.5 multiply_reduce_fusion.1
  269.5 102.7 %shard_map.155 = bf16[1664,768]{1,0:T(8,128)(2,1)S(1)} custom-call(bf16[768,2304]{1,0:T(8,128)(2,1)} %convolution_convert_fusion.1.refs_0_, bf16[768,768]{1,0:T(8,128)(2,1)S(1)} %convolution_convert_fusion.3.refs_1_, bf16[768,2304]{1,0:T(8,128)(2,1)} %convolution_convert_fusion.refs_2_, bf16[1152,768]{1,0:T(8,128)(2,1)S(1)} %convolution_convert_fusion.2.refs_3_, ...), custom_call_target="tpu_custom_call" | custom-call | tf_op jit(solution)/shard_map/pallas_call | solution.py:763
  372.1 0.6 fusion.32
  372.7 1.0 slice.198
  373.7 1.2 fusion.31
  374.9 0.5 copy-done.13
  375.4 1.1 add_convert_fusion.1
  376.5 1.3 pad_maximum_fusion.3
  377.8 1.3 pad_maximum_fusion.2
  (103 shorter events, 3.8 us)
Async XLA Ops:
  127.2 5.7 %copy-start.2 = (bf16[2,128,768]{2,1,0:T(8,128)(2,1)S(1)}, bf16[2,128,768]{2,1,0:T(8,128)(2,1)}, u32[]{:S(2)}) copy-start(bf16[2,128,768]{2,1,0:T(8,128)(2,1)} %param.9) | copy-start | bytes 1179652
  132.9 1.1 copy-start.18
  132.9 3.5 copy-start.16
  133.7 2.8 copy-start.28
  136.5 0.7 copy-start.31
  174.4 10.3 %all-to-all-start.1 = ((bf16[8,192,128]{2,1,0:T(8,128)(2,1)}), bf16[8,192,128]{2,1,0:T(8,128)(2,1)S(1)}, u32[]{:S(2)}, u32[]{:S(2)}) async-start(bf16[8,192,128]{2,1,0:T(8,128)(2,1)} %bitcast.112), calls=%async_computation.1 | async-start | bytes 786432 | tf_op jit(solution)/shard_map/all_to_all | solution.py:849
  185.1 2.1 copy-start.8
  185.1 2.3 copy-start.21
  185.2 2.3 copy-start.22
  185.2 2.5 copy-start.23
  187.2 5.3 %copy-start = (f32[256,768]{1,0:T(8,128)}, f32[256,768]{1,0:T(8,128)S(1)}, u32[]{:S(2)}) copy-start(f32[256,768]{1,0:T(8,128)S(1)} %get-tuple-element.71) | copy-start | bytes 2359300
  187.6 1.5 copy-start.3
  187.6 1.5 copy-start.10
  191.1 1.3 copy-start.24
  191.1 1.4 copy-start.26
  192.9 3.0 copy-start.5
  192.9 1.7 copy-start.7
  193.1 0.8 copy-start.14
  230.4 5.2 %copy-start.9 = (bf16[1,4,192,2,128]{4,3,2,1,0:T(2,128)(2,1)S(1)}, bf16[1,4,192,2,128]{4,3,2,1,0:T(2,128)(2,1)}, u32[]{:S(2)}) copy-start(bf16[1,4,192,2,128]{4,3,2,1,0:T(2,128)(2,1)} %copy-done.8) | copy-start | bytes 1179652
  230.4 5.2 %copy-start.15 = (bf16[256,768]{1,0:T(8,128)(2,1)S(1)}, bf16[256,768]{1,0:T(8,128)(2,1)}, u32[]{:S(2)}) copy-start(bf16[256,768]{1,0:T(8,128)(2,1)} %copy-done.14) | copy-start | bytes 1179652
  230.4 18.3 %all-to-all-start.3 = ((bf16[8,576,128]{2,1,0:T(8,128)(2,1)}), bf16[8,576,128]{2,1,0:T(8,128)(2,1)}, u32[]{:S(2)}, u32[]{:S(2)}) async-start(bf16[8,576,128]{2,1,0:T(8,128)(2,1)} %copy.54), calls=%async_computation.3 | async-start | bytes 2359296 | tf_op jit(solution)/shard_map/all_to_all | solution.py:849
  236.1 2.0 copy-start.1
  236.1 2.0 copy-start.4
  238.1 2.7 copy-start.25
  238.2 2.7 copy-start.27
  261.5 1.9 copy-start.19
  261.5 2.1 copy-start.20
  263.2 1.4 copy-start.17
  263.2 1.4 copy-start.30
  264.7 1.2 copy-start.29
  265.9 3.0 copy-start.12
  373.7 1.2 copy-start.6
  373.7 1.2 copy-start.11
  373.7 1.7 copy-start.13

commit v3 on v2

--- a/solution.py
+++ b/solution.py
@@ -486,8 +486,8 @@
 
 
 def gather_kernel(count, *refs):
-    parts, out = refs[:count], refs[count]
-    line_send, line_recv, send, recv, local = refs[count + 1 :]
+    parts, result, out = refs[:count], refs[count], refs[count + 1]
+    line_send, line_recv, send, recv, local, stored = refs[count + 2 :]
     depth, total, width = out.shape
     size = total // CTX
     me = Place()
@@ -503,6 +503,10 @@
     greet(me, depth)
     for keep in keeps:
         keep.wait()
+
+    def store(origin):
+        return pltpu.make_async_copy(out.at[origin], result.at[origin], stored.at[origin])
+
     mine = rows_at(me.piece() * size, size)
 
     def along(way, t):
@@ -538,6 +542,7 @@
         def _():
             along(way, 0).start()
 
+    store(me.z).start()
     for t in range(1, depth + 2):
         for way in (0, 1):
             if t < depth:
@@ -576,12 +581,16 @@
             @pl.when(comes(way, t))
             def _():
                 steps(way, t)[3]()
+                store(jnp.clip(me.z - t if way == 0 else me.z + t, 0, depth - 1)).start()
 
         for t in range(depth - 1):
 
             @pl.when(goes(way, t))
             def _():
                 along(way, t).wait_send()
+
+    for zz in range(depth):
+        store(zz).wait()
 
 
 def gather_packed(parts, width):
@@ -594,13 +603,17 @@
         in_specs=[pl.BlockSpec(memory_space=pl.ANY)] * len(parts),
         out_specs=pl.BlockSpec(memory_space=pl.ANY),
         scratch_shapes=[
+            pltpu.VMEM((depth, used, width), parts[0].dtype),
             dma((2, depth - 1)),
             dma((2, depth - 1)),
             dma((2 * (depth - 1), SPREAD)),
             dma((2 * (depth - 1), SPREAD)),
             dma((len(plan),)),
+            dma((depth,)),
         ],
-        compiler_params=pltpu.CompilerParams(collective_id=1, has_side_effects=True),
+        compiler_params=pltpu.CompilerParams(
+            collective_id=1, has_side_effects=True, vmem_limit_bytes=32 * 2**20
+        ),
     )(*parts)
 
 

time: 380 us -> 305 us (0.80)
  Pallas kernels: 255 us -> 177 us
  local copies, waits for them, and re-layouts: 36.2 us -> 40.4 us
    pallas_call x1, Pallas kernels: 124 us -> 46.6 us  [gather_packed(): pl.pallas_call(functools.partial(gather_kernel, len(parts)), out_shape=ja...]
    unnamed x68 -> x78, local copies, waits for them, and re-layouts: 6.21 us -> 13.6 us
  transfers between devices with their start and end apart: 2 -> 2, of which waited for: 2 -> 2; matrix products, arithmetic and copies ran while one was open for 3% -> 4% of each run, Pallas kernels for 0% -> 0%
where the time goes in v3:
time: 305 us; the launch traced here: 304 us
  Pallas kernels  177 us (58%)
  local copies, waits for them, and re-layouts  40.4 us (13%)
  blocking collectives  31.1 us (10%)
  matrix products  22.3 us (7%)
  other arithmetic  14.6 us (5%)
  starting transfers between devices  9.36 us (3%)
  waiting for transfers between devices  8.06 us (3%)
    pallas_call x1, Pallas kernels, reduce_packed(): pl.pallas_call(functools.partial(reduce_kernel, len(parts)), out_shape=ja...  102 us
    pallas_call x1, Pallas kernels, gather_packed(): pl.pallas_call(functools.partial(gather_kernel, len(parts)), out_shape=ja...  46.6 us
    all_to_all x2, blocking collectives, swap(): return lax.all_to_all(sent, 'ctx', split_axis=0, concat_axis=0, tiled=True)  31.1 us
    dot_general x12, matrix products, mm(): lax.dot_general(left, right, dims, preferred_element_type=jnp.float32)  22.3 us
    pallas_call x1, Pallas kernels, attend_back(): pl.pallas_call(attend_back_kernel, grid=(pairs, length // rows), in_specs...  15.4 us
    unnamed x78, local copies, waits for them, and re-layouts  13.6 us
    pallas_call x1, Pallas kernels, attend(): pl.pallas_call(attend_kernel, grid=(pairs, length // rows), in_specs=[par...  12.9 us
    all_to_all x2, starting transfers between devices, swap(): return lax.all_to_all(sent, 'ctx', split_axis=0, concat_axis=0, tiled=True)  9.36 us
  transfers between devices with their start and end apart: 2, of which 2 were waited for; matrix products, arithmetic and copies ran while one was open for 4% of the time, Pallas kernels for 0%

profile of v3, /device:TPU:17, one launch (start us, length us, event | category | flops | bytes accessed | tf_op | source)
XLA Modules:
  0.0 304.1 jit_solution(6393172800085526791)
XLA Ops:
  0.6 0.7 stack.56
  1.3 0.7 stack.57
  2.0 1.2 copy-done.1
  3.2 1.2 copy-done.2
  4.3 1.0 copy-done.3
  5.3 1.0 copy-done.4
  6.3 46.6 %shard_map.152 = bf16[4,1664,768]{2,1,0:T(8,128)(2,1)S(1)} custom-call(bf16[192,2304]{1,0:T(8,128)(2,1)S(1)} %copy-done.1, bf16[192,768]{1,0:T(8,128)(2,1)S(1)} %copy-done.4, bf16[192,2304]{1,0:T(8,128)(2,1)S(1)} %copy-done.2, bf16[288,768]{1,0:T(8,128)(2,1)S(1)} %copy-done.3, bf16[32,768]{1,0:T(8,128)(2,1)S(1)} %fusion.17.refs_4_), custom_call_target="tpu_custom_call" | custom-call | tf_op jit(solution)/shard_map/pallas_call | solution.py:600
  53.0 2.5 fusion.30
  55.4 3.1 %copy-done = bf16[4,1664,768]{2,1,0:T(8,128)(2,1)} copy-done((bf16[4,1664,768]{2,1,0:T(8,128)(2,1)}, bf16[4,1664,768]{2,1,0:T(8,128)(2,1)S(1)}, u32[]{:S(2)}) %copy-start) | copy-done | bytes 10223640
  59.2 0.4 copy-done.23
  59.6 2.4 fusion.3
  62.3 0.5 copy-done.36
  63.6 2.0 maximum_bitcast_fusion
  65.7 0.2 copy.46
  66.0 19.0 %all_to_all.20 = bf16[8,592,128]{2,1,0:T(8,128)(2,1)S(1)} all-to-all(bf16[8,592,128]{2,1,0:T(8,128)(2,1)S(1)} %pad_maximum_fusion.8), channel_id=1, replica_groups=mesh['ctx'=8,'wsh'=4] {'ctx'}, dimensions={0} | all-to-all | bytes 2424832 | tf_op jit(solution)/shard_map/all_to_all | solution.py:862
  85.0 0.3 copy.79
  86.2 12.9 %shard_map.153 = (f32[3,64,1024]{2,1,0:T(8,128)S(1)}, f32[3,1024,1024]{2,1,0:T(8,128)}) custom-call(bf16[3,64,1024]{2,1,0:T(8,128)(2,1)S(1)} %reshape.315.q_ref, bf16[3,64,1024]{2,1,0:T(8,128)(2,1)S(1)} %reshape.316.k_ref, bf16[3,64,1024]{2,1,0:T(8,128)(2,1)S(1)} %reshape.317.v_ref, f32[1024,1]{1,0:T(8,128)S(1)} %copy.48.mask_ref), custom_call_target="tpu_custom_call" | custom-call | flops 805306368 | bytes 12582912 | tf_op jit(solution)/shard_map/pallas_call | solution.py:289
  99.2 0.8 copy.81
  100.0 4.2 %all-to-all-start.1 = ((bf16[8,192,128]{2,1,0:T(8,128)(2,1)}), bf16[8,192,128]{2,1,0:T(8,128)(2,1)S(1)}, u32[]{:S(2)}, u32[]{:S(2)}) async-start(bf16[8,192,128]{2,1,0:T(8,128)(2,1)} %bitcast.112), calls=%async_computation.1 | async-start | bytes 786432 | tf_op jit(solution)/shard_map/all_to_all | solution.py:862
  104.3 2.8 slice.151
  107.2 3.2 %all-to-all-done.1 = bf16[8,192,128]{2,1,0:T(8,128)(2,1)S(1)} async-done(((bf16[8,192,128]{2,1,0:T(8,128)(2,1)}), bf16[8,192,128]{2,1,0:T(8,128)(2,1)S(1)}, u32[]{:S(2)}, u32[]{:S(2)}) %all-to-all-start.1) | async-done | bytes 393248 | tf_op jit(solution)/shard_map/all_to_all | solution.py:862
  110.3 0.4 copy.50
  110.8 2.0 fusion.36
  113.2 1.1 fusion.1
  114.4 0.3 copy-done.8
  114.8 1.9 fusion.9
  116.7 1.2 multiply_reduce_fusion
  118.2 0.3 fusion.29
  118.7 0.7 copy-done.19
  119.5 0.8 copy-done.12
  120.2 1.3 convolution_convert_fusion.4
  121.5 1.8 reshape_broadcast_in_dim.3
  123.3 1.0 copy.52
  124.4 12.2 %all_to_all.21 = bf16[8,192,128]{2,1,0:T(8,128)(2,1)S(1)} all-to-all(bf16[8,192,128]{2,1,0:T(8,128)(2,1)S(1)} %bitcast.136), channel_id=1, replica_groups=mesh['ctx'=8,'wsh'=4] {'ctx'}, dimensions={0} | all-to-all | bytes 786432 | tf_op jit(solution)/shard_map/all_to_all | solution.py:862
  136.5 1.0 copy.53
  137.5 1.2 reshape.327.do_ref
  138.7 15.4 %shard_map.154 = (f32[3,64,1024]{2,1,0:T(8,128)S(1)}, f32[3,64,1024]{2,1,0:T(8,128)S(1)}, f32[3,64,1024]{2,1,0:T(8,128)S(1)}) custom-call(bf16[3,64,1024]{2,1,0:T(8,128)(2,1)S(1)} %reshape.315.q_ref, bf16[3,64,1024]{2,1,0:T(8,128)(2,1)S(1)} %reshape.316.k_ref, bf16[3,64,1024]{2,1,0:T(8,128)(2,1)S(1)} %reshape.317.v_ref, ...), custom_call_target="tpu_custom_call" | custom-call | flops 1610612736 | bytes 12582912 | tf_op jit(solution)/shard_map/pallas_call | solution.py:332
  154.5 0.3 copy.61
  154.8 1.2 copy.54
  156.0 5.1 %all-to-all-start.3 = ((bf16[8,576,128]{2,1,0:T(8,128)(2,1)}), bf16[8,576,128]{2,1,0:T(8,128)(2,1)}, u32[]{:S(2)}, u32[]{:S(2)}) async-start(bf16[8,576,128]{2,1,0:T(8,128)(2,1)} %copy.54), calls=%async_computation.3 | async-start | bytes 2359296 | tf_op jit(solution)/shard_map/all_to_all | solution.py:862
  161.1 0.5 convolution_convert_fusion.3.refs_1_
  161.7 2.0 convolution_convert_fusion.2.refs_3_
  163.8 2.7 fusion.4
  166.4 3.0 convolution_convert_fusion.refs_2_
  169.4 4.9 %all-to-all-done.3 = bf16[8,576,128]{2,1,0:T(8,128)(2,1)} async-done(((bf16[8,576,128]{2,1,0:T(8,128)(2,1)}), bf16[8,576,128]{2,1,0:T(8,128)(2,1)}, u32[]{:S(2)}, u32[]{:S(2)}) %all-to-all-start.3) | async-done | bytes 1179680 | tf_op jit(solution)/shard_map/all_to_all | solution.py:862
  174.3 4.1 %fusion.28 = (f32[3,4,192,2,128]{4,3,2,1,0:T(2,128)S(1)}, bf16[3,4,192,2,128]{4,3,2,1,0:T(2,128)(2,1)}) fusion(bf16[2,4,3,192,128]{4,3,2,1,0:T(8,128)(2,1)} %bitcast.32), kind=kLoop, calls=%fused_computation.102 | loop fusion | flops 589824 | bytes 4718592 | tf_op jit(solution)/shard_map/convert_element_type | solution.py:926
  178.4 1.3 fusion.33
  179.7 2.7 reshape_squeeze.8
  182.4 1.3 slice.188
  183.6 0.8 copy.80
  184.4 2.6 reshape_squeeze.9
  187.1 1.8 subtract_convert_fusion.1
  189.2 1.0 copy-done.22
  190.3 1.2 multiply_reduce_fusion.2
  191.5 2.9 convolution_convert_fusion.1.refs_0_
  194.5 0.5 multiply_reduce_fusion.1
  195.0 102.1 %shard_map.155 = bf16[1664,768]{1,0:T(8,128)(2,1)S(1)} custom-call(bf16[768,2304]{1,0:T(8,128)(2,1)} %convolution_convert_fusion.1.refs_0_, bf16[768,768]{1,0:T(8,128)(2,1)S(1)} %convolution_convert_fusion.3.refs_1_, bf16[768,2304]{1,0:T(8,128)(2,1)} %convolution_convert_fusion.refs_2_, bf16[1152,768]{1,0:T(8,128)(2,1)S(1)} %convolution_convert_fusion.2.refs_3_, ...), custom_call_target="tpu_custom_call" | custom-call | tf_op jit(solution)/shard_map/pallas_call | solution.py:776
  297.1 0.6 fusion.32
  297.7 1.0 slice.198
  298.7 1.2 fusion.31
  299.9 0.5 copy-done.18
  300.4 1.1 add_convert_fusion.1
  301.5 1.3 pad_maximum_fusion.3
  302.8 1.3 pad_maximum_fusion.2
  (113 shorter events, 4.6 us)
Async XLA Ops:
  2.0 1.2 copy-start.1
  3.2 1.2 copy-start.2
  4.3 1.0 copy-start.3
  5.3 1.0 copy-start.4
  52.9 5.6 %copy-start = (bf16[4,1664,768]{2,1,0:T(8,128)(2,1)}, bf16[4,1664,768]{2,1,0:T(8,128)(2,1)S(1)}, u32[]{:S(2)}) copy-start(bf16[4,1664,768]{2,1,0:T(8,128)(2,1)S(1)} %shard_map.152) | copy-start | bytes 30670852
  53.0 5.6 %copy-start.7 = (bf16[2,128,768]{2,1,0:T(8,128)(2,1)S(1)}, bf16[2,128,768]{2,1,0:T(8,128)(2,1)}, u32[]{:S(2)}) copy-start(bf16[2,128,768]{2,1,0:T(8,128)(2,1)} %param.9) | copy-start | bytes 1179652
  58.5 1.1 copy-start.23
  58.5 3.5 %copy-start.21 = (bf16[4,192,768]{2,1,0:T(8,128)(2,1)}, bf16[4,192,768]{2,1,0:T(8,128)(2,1)S(1)}, u32[]{:S(2)}) copy-start(bf16[4,192,768]{2,1,0:T(8,128)(2,1)S(1)} %get-tuple-element.30) | copy-start | bytes 3538948
  59.2 2.8 copy-start.33
  62.1 0.7 copy-start.36
  100.0 10.3 %all-to-all-start.1 = ((bf16[8,192,128]{2,1,0:T(8,128)(2,1)}), bf16[8,192,128]{2,1,0:T(8,128)(2,1)S(1)}, u32[]{:S(2)}, u32[]{:S(2)}) async-start(bf16[8,192,128]{2,1,0:T(8,128)(2,1)} %bitcast.112), calls=%async_computation.1 | async-start | bytes 786432 | tf_op jit(solution)/shard_map/all_to_all | solution.py:862
  110.7 2.1 copy-start.13
  110.8 2.3 copy-start.26
  110.8 2.3 copy-start.27
  110.8 2.5 copy-start.28
  112.8 5.3 %copy-start.5 = (f32[256,768]{1,0:T(8,128)}, f32[256,768]{1,0:T(8,128)S(1)}, u32[]{:S(2)}) copy-start(f32[256,768]{1,0:T(8,128)S(1)} %get-tuple-element.71) | copy-start | bytes 2359300
  113.2 1.5 copy-start.8
  113.2 1.5 copy-start.15
  116.7 1.3 copy-start.29
  116.7 1.5 copy-start.31
  118.5 3.0 copy-start.10
  118.5 1.7 copy-start.12
  118.7 0.8 copy-start.19
  156.0 5.1 %copy-start.14 = (bf16[1,4,192,2,128]{4,3,2,1,0:T(2,128)(2,1)S(1)}, bf16[1,4,192,2,128]{4,3,2,1,0:T(2,128)(2,1)}, u32[]{:S(2)}) copy-start(bf16[1,4,192,2,128]{4,3,2,1,0:T(2,128)(2,1)} %copy-done.13) | copy-start | bytes 1179652
  156.0 5.1 %copy-start.20 = (bf16[256,768]{1,0:T(8,128)(2,1)S(1)}, bf16[256,768]{1,0:T(8,128)(2,1)}, u32[]{:S(2)}) copy-start(bf16[256,768]{1,0:T(8,128)(2,1)} %copy-done.19) | copy-start | bytes 1179652
  156.0 18.3 %all-to-all-start.3 = ((bf16[8,576,128]{2,1,0:T(8,128)(2,1)}), bf16[8,576,128]{2,1,0:T(8,128)(2,1)}, u32[]{:S(2)}, u32[]{:S(2)}) async-start(bf16[8,576,128]{2,1,0:T(8,128)(2,1)} %copy.54), calls=%async_computation.3 | async-start | bytes 2359296 | tf_op jit(solution)/shard_map/all_to_all | solution.py:862
  161.7 2.0 copy-start.6
  161.7 2.0 copy-start.9
  163.7 2.7 copy-start.30
  163.8 2.7 copy-start.32
  187.1 1.9 copy-start.24
  187.1 2.1 copy-start.25
  188.9 1.4 copy-start.22
  188.9 1.4 copy-start.35
  190.3 1.2 copy-start.34
  191.5 2.9 copy-start.17
  298.7 1.2 copy-start.11
  298.7 1.2 copy-start.16
  298.7 1.7 copy-start.18
